TPU v7x, 256 devices: a whole 4x4x8 slice. The times are simulated.
256 devices in a mesh: az: 128 (over z, x, y_hi, core), dep: 2 (over y_lo).
Axes of the slice: x: 4, y: 4 (y_hi: 2, y_lo: 2; y = y_hi * 2 + y_lo), z: 8, core: 2. Of those that a mesh axis runs over, the one named last changes fastest.
Arguments:
- field: float32 [8192, 2, 1024], P('az', None, 'dep'), may hold values from -6 to 6
- brick_speed: bfloat16 [32768, 1024], P('az', 'dep'), may hold values from -40 to 40
- send_index: int32 [128, 128, 32], P('az'), may hold values from 0 to 255
- send_count: int32 [128, 128], P('az'), may hold values from 0 to 32, as said below
- weights: bfloat16 [8192, 4, 4096], P('az'), may hold values from 0 to 1, as said below
- propagator: bfloat16 [2, 2, 1024, 1024], replicated, may hold values from -1 to 1
Outputs:
- pressure: float32 [8192, 2, 1024], P('az', None, 'dep')
Inputs may be any that keep to these rules, and one draw needn't show every extreme that they name: `send_count`: 32 or fewer columns from one brick to one sector; one sector receives 32 from every brick. Nonnegative interpolation weights.
All inputs are finite; a program needn't handle non-finite values.
Results may differ from a plain program's by a relative error of at most 0.025.
Values may be sent and summed in bfloat16 or wider, within the bound.
No kernel may reach another device: no remote copies, remote signals or barrier semaphores. Data moves between devices by JAX's collectives and lax.ppermute only.
A program may use at most 64 MiB of HBM per device.

v0:
```python
import math

import jax
import jax.numpy as jnp
from jax import lax
from jax.experimental import pallas as pl
from jax.experimental.pallas import tpu as pltpu
from jax.sharding import Mesh, PartitionSpec as P

angle_rate = 200.0 / 1500.0
couple_real = 0.1
couple_imag = 0.15

AXES = ("z", "x", "yh", "c", "yl")
SECTOR = ("z", "x", "yh", "c")
SIZES = (8, 4, 2, 2, 2)
HALO = 8
ROWS = 32
EXT = ROWS + 2 * HALO
NZ = 1024
STEPS = 4
FACTORS = 2
RING = 256
VMEM = pl.BlockSpec(memory_space=pltpu.VMEM)
SMEM = pl.BlockSpec(memory_space=pltpu.SMEM)


def turn_code(speed):
    turns = speed * (-angle_rate / (2.0 * math.pi))
    code = jnp.round((turns - jnp.round(turns)) * 65536.0).astype(jnp.int32)
    return jnp.where(code > 32767, -32768, code)


def cos_sin(code):
    quadrant = (code + 8192) >> 14
    part = (code - (quadrant << 14)).astype(jnp.float32) * (1.0 / 16384.0)
    square = part * part
    h = math.pi / 2
    sine = part * (h + square * (-(h**3) / 6 + square * (h**5 / 120 - square * (h**7 / 5040))))
    cosine = 1.0 + square * (
        -(h**2) / 2 + square * (h**4 / 24 + square * (-(h**6) / 720 + square * (h**8 / 40320)))
    )
    odd = (quadrant & 1) == 1
    first = jnp.where(odd, sine, cosine)
    second = jnp.where(odd, cosine, sine)
    first = jnp.where(((quadrant + 1) & 2) == 2, -first, first)
    second = jnp.where((quadrant & 2) == 2, -second, second)
    return first, second


def march_kernel(
    side, code, code_left, code_right, field, field_left, field_right, factors_hbm, keep, send, *scratch
):
    state, padded, rounded, codes, factors, arrived = scratch
    copies = [pltpu.make_async_copy(factors_hbm.at[i], factors.at[i], arrived.at[i]) for i in range(FACTORS)]
    for copy in copies:
        copy.start()
    state[:, 0:HALO] = field_left[...]
    state[:, HALO : HALO + ROWS] = field[...]
    state[:, HALO + ROWS : EXT] = field_right[...]
    padded[:, 0:HALO] = jnp.zeros((2, HALO, NZ), jnp.float32)
    padded[:, HALO + EXT :] = jnp.zeros((2, HALO, NZ), jnp.float32)
    edge, body = STEPS * HALO, STEPS * ROWS
    for chunk in range(NZ // 128):
        lanes = slice(chunk * 128, (chunk + 1) * 128)
        codes[chunk, 0:edge] = code_left[:, lanes].astype(jnp.int32)
        codes[chunk, edge : edge + body] = ((code[:, lanes] + 32768) & 65535) - 32768
        codes[chunk, edge + body :] = code_right[:, lanes].astype(jnp.int32)
    for step in range(STEPS):
        for chunk in range(NZ // 128):
            lanes = slice(chunk * 128, (chunk + 1) * 128)
            cosine, sine = cos_sin(codes[chunk, pl.ds(step, EXT, stride=STEPS), :])
            real = state[0, :, lanes]
            imag = state[1, :, lanes]
            padded[0, HALO : HALO + EXT, lanes] = real * cosine - imag * sine
            padded[1, HALO : HALO + EXT, lanes] = real * sine + imag * cosine
        laplace = []
        for part in range(2):
            near = padded[part, HALO - 1 : HALO - 1 + EXT] + padded[part, HALO + 1 : HALO + 1 + EXT]
            far = padded[part, HALO - 2 : HALO - 2 + EXT] + padded[part, HALO + 2 : HALO + 2 + EXT]
            centre = padded[part, HALO : HALO + EXT]
            laplace.append((16.0 * near - far - 30.0 * centre) * (1.0 / 12.0))
        rounded[0:EXT] = (
            padded[0, HALO : HALO + EXT] + couple_real * laplace[0] - couple_imag * laplace[1]
        ).astype(jnp.bfloat16)
        rounded[EXT : 2 * EXT] = (
            padded[1, HALO : HALO + EXT] + couple_real * laplace[1] + couple_imag * laplace[0]
        ).astype(jnp.bfloat16)
        for factor in range(FACTORS):
            if step == 0:
                copies[factor].wait()
            left = rounded[...]
            for column in range(0, NZ, 256):
                by_real = jnp.dot(
                    left, factors[factor, 0, :, column : column + 256], preferred_element_type=jnp.float32
                )
                by_imag = jnp.dot(
                    left, factors[factor, 1, :, column : column + 256], preferred_element_type=jnp.float32
                )
                state[0, :, column : column + 256] = by_real[:EXT] - by_imag[EXT:]
                state[1, :, column : column + 256] = by_imag[:EXT] + by_real[EXT:]
            if factor + 1 < FACTORS:
                rounded[0:EXT] = state[0].astype(jnp.bfloat16)
                rounded[EXT : 2 * EXT] = state[1].astype(jnp.bfloat16)
    low = state[:, HALO : HALO + ROWS, 0 : NZ // 2]
    high = state[:, HALO : HALO + ROWS, NZ // 2 :]
    first = side[0] == 0
    keep[...] = jnp.where(first, low, high)
    send[...] = jnp.where(first, high, low).astype(jnp.bfloat16)


def march(side, code, code_left, code_right, field, field_left, field_right, factors):
    half = (2, ROWS, NZ // 2)
    return pl.pallas_call(
        march_kernel,
        out_shape=(jax.ShapeDtypeStruct(half, jnp.float32), jax.ShapeDtypeStruct(half, jnp.bfloat16)),
        in_specs=[SMEM] + [VMEM] * 6 + [pl.BlockSpec(memory_space=pl.ANY)],
        out_specs=(VMEM, VMEM),
        scratch_shapes=[
            pltpu.VMEM((2, EXT, NZ), jnp.float32),
            pltpu.VMEM((2, EXT + 2 * HALO, NZ), jnp.float32),
            pltpu.VMEM((2 * EXT, NZ), jnp.bfloat16),
            pltpu.VMEM((NZ // 128, STEPS * EXT, 128), jnp.int32),
            pltpu.VMEM((FACTORS, 2, NZ, NZ), jnp.bfloat16),
            pltpu.SemaphoreType.DMA((FACTORS,)),
        ],
        compiler_params=pltpu.CompilerParams(vmem_limit_bytes=40 * 1024 * 1024),
        cost_estimate=pl.CostEstimate(
            flops=2 * 8 * 2 * EXT * NZ * 2 * NZ, bytes_accessed=10 * 1024 * 1024, transcendentals=0
        ),
        name="march",
    )(side, code, code_left, code_right, field, field_left, field_right, factors)


def swap_dep(value):
    return lax.ppermute(value, "yl", [(0, 1), (1, 0)])


def ring_step(value, shift):
    return lax.ppermute(value, AXES, [(i, (i + shift) % RING) for i in range(RING)])


def own_rows_all_depths(first, value, dim, depth_dim):
    top = lax.slice_in_dim(value, 0, ROWS, axis=dim)
    bottom = lax.slice_in_dim(value, ROWS, 2 * ROWS, axis=dim)
    mine = jnp.where(first, top, bottom)
    other = swap_dep(jnp.where(first, bottom, top))
    return jnp.where(
        first, jnp.concatenate([mine, other], depth_dim), jnp.concatenate([other, mine], depth_dim)
    )


def with_halo(value, width):
    before = ring_step(value[:, -width:], 1)
    after = ring_step(value[:, :width], -1)
    return before, after


PLANE = 8
SLOTS = 512
BCOL = 256
CAP = 32
DEPTH = NZ // 2
EARLY = (0, -1, 1, -2, 2)
LATE = (-3, 3, 4)


def sort_kernel(weights, out):
    rows = weights.shape[0] * STEPS
    lane = lax.broadcasted_iota(jnp.int32, (rows, 128), 1)
    for pair in range(4):
        for x in range(4):
            both = []
            for z in (2 * pair, 2 * pair + 1):
                start = z * SLOTS + x * 128
                both.append(weights[:, :, start : start + 128].astype(jnp.float32).reshape(rows, 128))
            even, odd = both
            out[2 * x, :, pair * 128 : pair * 128 + 128] = jnp.where(
                lane < 64, even, pltpu.roll(odd, 64, 1)
            ).astype(jnp.bfloat16)
            out[2 * x + 1, :, pair * 128 : pair * 128 + 128] = jnp.where(
                lane < 64, pltpu.roll(even, 64, 1), odd
            ).astype(jnp.bfloat16)


def sort_weights(weights):
    block = 16
    return pl.pallas_call(
        sort_kernel,
        out_shape=jax.ShapeDtypeStruct((PLANE, 2 * ROWS * STEPS, SLOTS), jnp.bfloat16),
        grid=(2 * ROWS // block,),
        in_specs=[pl.BlockSpec((block, STEPS, 8 * SLOTS), lambda i: (i, 0, 0))],
        out_specs=pl.BlockSpec((PLANE, block * STEPS, SLOTS), lambda i: (0, i, 0)),
        compiler_params=pltpu.CompilerParams(vmem_limit_bytes=12 * 1024 * 1024),
        cost_estimate=pl.CostEstimate(flops=0, bytes_accessed=4 * 1024 * 1024, transcendentals=0),
        name="sort",
    )(weights)


def pack_kernel(place, *refs):
    pieces, (mine, other) = refs[:-2], refs[-2:]
    z, core = place[0], place[1]
    line = lax.broadcasted_iota(jnp.int32, (16, BCOL), 0)
    column = lax.broadcasted_iota(jnp.int32, (BCOL // 2, 2 * BCOL), 0)
    for brick in range(len(pieces) // 2):
        low, high = pieces[2 * brick], pieces[2 * brick + 1]
        table = low[BCOL // 2 :, 0:BCOL].astype(jnp.float32)
        index = jnp.concatenate(
            [
                jnp.sum(jnp.where(line == z * 2 + target, table, 0.0), axis=0, keepdims=True)
                for target in (core, 1 - core)
            ],
            axis=1,
        ).astype(jnp.int32)
        total = None
        for half, ref in enumerate((low, high)):
            onehot = jnp.where(column + half * (BCOL // 2) == index, 1.0, 0.0).astype(jnp.bfloat16)
            part = lax.dot_general(
                onehot, ref[0 : BCOL // 2, :], (((0,), (0,)), ((), ())), preferred_element_type=jnp.float32
            )
            total = part if total is None else total + part
        total = total.astype(jnp.bfloat16)
        span = slice(brick * CAP, (brick + 1) * CAP)
        mine[:, span, :] = total[:BCOL].reshape(PLANE, CAP, DEPTH)
        other[:, span, :] = total[BCOL:].reshape(PLANE, CAP, DEPTH)


def pack(place, pieces):
    bricks = len(pieces) // 2
    shape = jax.ShapeDtypeStruct((PLANE, bricks * CAP, DEPTH), jnp.bfloat16)
    return pl.pallas_call(
        pack_kernel,
        out_shape=(shape, shape),
        in_specs=[SMEM] + [VMEM] * len(pieces),
        out_specs=(VMEM, VMEM),
        compiler_params=pltpu.CompilerParams(vmem_limit_bytes=12 * 1024 * 1024),
        cost_estimate=pl.CostEstimate(
            flops=bricks * 2 * 512 * 256 * 512, bytes_accessed=bricks * 768 * 1024, transcendentals=0
        ),
        name="pack",
    )(place, *pieces)


def partial_kernel(place, *refs):
    groups, (weights, out, packed) = refs[:4], refs[4:]
    z, core = place[0], place[1]
    for group, ref in enumerate(groups):
        from_core = core if group < 2 else 1 - core
        for brick, shift in enumerate(LATE if group % 2 else EARLY):
            from_z = lax.rem(z + shift + 8, 8)
            start = pl.multiple_of((from_z * 2 + from_core) * CAP, CAP)
            packed[:, pl.ds(start, CAP), :] = ref[:, brick * CAP : (brick + 1) * CAP, :]
    for sector in range(PLANE):
        code = turn_code(jnp.dot(weights[sector], packed[sector], preferred_element_type=jnp.float32))
        out[sector] = code.astype(jnp.int16).reshape(2, STEPS * ROWS, DEPTH)


def partial_codes(place, groups, weights):
    return pl.pallas_call(
        partial_kernel,
        out_shape=jax.ShapeDtypeStruct((PLANE, 2, STEPS * ROWS, DEPTH), jnp.int16),
        in_specs=[SMEM] + [VMEM] * 5,
        out_specs=VMEM,
        scratch_shapes=[pltpu.VMEM((PLANE, SLOTS, DEPTH), jnp.bfloat16)],
        compiler_params=pltpu.CompilerParams(vmem_limit_bytes=20 * 1024 * 1024),
        cost_estimate=pl.CostEstimate(flops=2 * 537_000_000, bytes_accessed=8 * 1024 * 1024, transcendentals=0),
        name="partial",
    )(place, *groups, weights)


def sum_kernel(parts, out):
    for half in range(2):
        total = parts[0, half].astype(jnp.int32)
        for source in range(1, PLANE):
            total = total + parts[source, half].astype(jnp.int32)
        out[:, half * DEPTH : (half + 1) * DEPTH] = total


def sum_codes(parts):
    return pl.pallas_call(
        sum_kernel,
        out_shape=jax.ShapeDtypeStruct((STEPS * ROWS, NZ), jnp.int32),
        in_specs=[VMEM],
        out_specs=VMEM,
        compiler_params=pltpu.CompilerParams(vmem_limit_bytes=12 * 1024 * 1024),
        cost_estimate=pl.CostEstimate(flops=2_000_000, bytes_accessed=2_500_000, transcendentals=0),
        name="sums",
    )(parts)


def edge_codes(parts):
    code = parts.astype(jnp.int32).sum(0)
    code = jnp.concatenate([code[0], code[1]], 1)
    return (((code + 32768) & 65535) - 32768).astype(jnp.int16)


def z_ring(value, shift):
    return lax.ppermute(value, "z", [(i, (i + shift) % 8) for i in range(8)])


def swap_core(value):
    return lax.ppermute(value, "c", [(0, 1), (1, 0)])


def gather_bricks(low, high):
    pieces = {(0, 0): low, (0, 1): high}
    for step in range(1, 4):
        for half in range(2):
            for way in (-1, 1):
                pieces[way * step, half] = z_ring(pieces[way * (step - 1), half], -way)
    pieces[4, 0] = z_ring(pieces[-3, 0], 1)
    pieces[4, 1] = z_ring(pieces[3, 1], -1)
    return pieces


def per_device(field, brick_speed, send_index, send_count, weights, propagator):
    first = lax.axis_index("yl") == 0
    moved = sort_weights(weights)
    moved = lax.all_to_all(moved, ("x", "yh"), split_axis=0, concat_axis=0, tiled=True)

    chosen = send_index[0]
    slots = lax.broadcasted_iota(jnp.int32, chosen.shape, 1)
    chosen = jnp.where(slots < send_count[0][:, None], chosen, -1).astype(jnp.bfloat16)
    chosen = chosen.reshape(8, 8, 2, CAP).transpose(0, 2, 1, 3).reshape(16, BCOL)
    chosen = jnp.pad(chosen, ((0, 0), (0, DEPTH - BCOL)))
    low = jnp.concatenate([brick_speed[: BCOL // 2], chosen])
    pieces = gather_bricks(low, brick_speed[BCOL // 2 :])
    place = jnp.stack([lax.axis_index("z"), lax.axis_index("c")]).astype(jnp.int32)

    own = own_rows_all_depths(first, field.transpose(1, 0, 2), 1, 2)
    own_left, own_right = with_halo(own, HALO)

    mine_early, other_early = pack(place, [pieces[shift, half] for shift in EARLY for half in range(2)])
    other_early = swap_core(other_early)
    late = [pieces[shift, half] for shift in LATE for half in range(2)]
    late, own, own_left, own_right = lax.optimization_barrier((late, own, own_left, own_right))
    mine_late, other_late = pack(place, late)
    other_late = swap_core(other_late)
    parts = partial_codes(place, (mine_early, mine_late, other_early, other_late), moved)
    parts = lax.all_to_all(
        parts.reshape(2 * PLANE, STEPS * ROWS, DEPTH), ("x", "yh", "yl"), split_axis=0, concat_axis=0, tiled=True
    ).reshape(PLANE, 2, STEPS * ROWS, DEPTH)
    edge = STEPS * HALO
    code_left = ring_step(edge_codes(parts[:, :, -edge:]), 1)
    code_right = ring_step(edge_codes(parts[:, :, :edge]), -1)
    code = sum_codes(parts)

    side = jnp.where(first, 0, 1).astype(jnp.int32).reshape(1)
    keep, send = march(side, code, code_left, code_right, own, own_left, own_right, propagator)
    other = swap_dep(send).astype(jnp.float32)
    out = jnp.where(first, jnp.concatenate([keep, other], 1), jnp.concatenate([other, keep], 1))
    return out.transpose(1, 0, 2)


def solution(mesh):
    inner = Mesh(mesh.devices.reshape(SIZES), AXES)
    placed = (
        P(SECTOR, None, "yl"),
        P(SECTOR, "yl"),
        P(SECTOR, None, None),
        P(SECTOR, None),
        P(SECTOR, None, None),
        P(),
    )
    return jax.shard_map(
        per_device, mesh=inner, in_specs=placed, out_specs=P(SECTOR, None, "yl"), check_vma=False
    )
```

profile of v0, /device:TPU:8, one launch (start us, length us, event | category | flops | bytes accessed | tf_op | source)
XLA Modules:
  0.0 144.1 jit_solution(13667904969243318719)
XLA Ops:
  0.0 1.0 fusion.12
  1.0 0.8 copy.11
  2.4 1.3 reduce.3
  4.1 2.0 %collective-permute-start = (bf16[144,512]{1,0:T(8,128)(2,1)S(1)}, bf16[144,512]{1,0:T(8,128)(2,1)S(1)}, u32[]{:S(2)}, u32[]{:S(2)}) collective-permute-start(bf16[144,512]{1,0:T(8,128)(2,1)S(1)} %fusion.2.refs_0_), channel_id=1, source_target_pairs={{0,32},{32,64},{64,96},{96,128},{128,160},{160,192},{192,224},{224... | collective-permute-start | bytes 442376 | tf_op jit(solution)/shard_map/ppermute | solution.py:298
  6.1 4.0 %collective-permute-start.2 = (bf16[144,512]{1,0:T(8,128)(2,1)S(1)}, bf16[144,512]{1,0:T(8,128)(2,1)S(1)}, u32[]{:S(2)}, u32[]{:S(2)}) collective-permute-start(bf16[144,512]{1,0:T(8,128)(2,1)S(1)} %fusion.2.refs_0_), channel_id=1, source_target_pairs={{0,224},{32,0},{64,32},{96,64},{128,96},{160,128},{192,160},{224,1... | collective-permute-start | bytes 442376 | tf_op jit(solution)/shard_map/ppermute | solution.py:298
  10.1 1.9 %collective-permute-start.3 = (bf16[128,512]{1,0:T(8,128)(2,1)S(1)}, bf16[128,512]{1,0:T(8,128)(2,1)S(1)}, u32[]{:S(2)}, u32[]{:S(2)}) collective-permute-start(bf16[128,512]{1,0:T(8,128)(2,1)S(1)} %get-tuple-element.41.refs_1_), channel_id=1, source_target_pairs={{0,224},{32,0},{64,32},{96,64},{128,96},{160,128},{192,160},{224,1... | collective-permute-start | bytes 393224 | tf_op jit(solution)/shard_map/ppermute | solution.py:298
  12.1 1.6 %copy-done = bf16[64,4,4096]{2,1,0:T(4,128)(2,1)S(1)} copy-done((bf16[64,4,4096]{2,1,0:T(4,128)(2,1)S(1)}, bf16[64,4,4096]{2,1,0:T(4,128)(2,1)}, u32[]{:S(2)}) %copy-start) | copy-done | bytes 2097176
  13.7 2.4 %sort.1 = bf16[8,256,512]{2,1,0:T(8,128)(2,1)} custom-call(bf16[64,4,4096]{2,1,0:T(4,128)(2,1)S(1)} %copy-done), custom_call_target="tpu_custom_call" | custom-call | bytes 4194304 | tf_op jit(solution)/shard_map/sort/pallas_call | solution.py:188
  16.2 6.2 %all-to-all-start = ((bf16[8,256,512]{2,1,0:T(8,128)(2,1)}), bf16[8,256,512]{2,1,0:T(8,128)(2,1)S(1)}, u32[]{:S(2)}, u32[]{:S(2)}) async-start(bf16[8,256,512]{2,1,0:T(8,128)(2,1)} %sort.1), calls=%async_computation | async-start | bytes 4194304 | tf_op jit(solution)/shard_map/all_to_all | solution.py:319
  22.4 3.2 %collective-permute-start.7 = (bf16[128,512]{1,0:T(8,128)(2,1)S(1)}, bf16[128,512]{1,0:T(8,128)(2,1)S(1)}, u32[]{:S(2)}, u32[]{:S(2)}) collective-permute-start(bf16[128,512]{1,0:T(8,128)(2,1)S(1)} %collective-permute-done.3.refs_5_), channel_id=1, source_target_pairs={{0,224},{32,0},{64,32},{96,64},{128,96},{160,128},{192,160},{224,1... | collective-permute-start | bytes 393224 | tf_op jit(solution)/shard_map/ppermute | solution.py:298
  26.3 3.3 %collective-permute-start.6 = (bf16[144,512]{1,0:T(8,128)(2,1)S(1)}, bf16[144,512]{1,0:T(8,128)(2,1)S(1)}, u32[]{:S(2)}, u32[]{:S(2)}) collective-permute-start(bf16[144,512]{1,0:T(8,128)(2,1)S(1)} %collective-permute-done.2.refs_4_), channel_id=1, source_target_pairs={{0,224},{32,0},{64,32},{96,64},{128,96},{160,128},{192,160},{224,1... | collective-permute-start | bytes 442376 | tf_op jit(solution)/shard_map/ppermute | solution.py:298
  30.4 1.3 collective-permute-start.14
  34.9 0.9 copy-done.10
  35.8 0.9 copy-done.15
  36.7 0.9 copy-done.17
  37.6 0.9 copy-done.19
  38.5 0.9 copy-done.21
  39.5 0.9 copy-done.23
  40.4 0.9 copy-done.25
  41.3 0.9 copy-done.27
  42.2 0.9 copy-done.29
  43.1 2.1 %pack.2 = (bf16[8,160,512]{2,1,0:T(8,128)(2,1)S(1)}, bf16[8,160,512]{2,1,0:T(8,128)(2,1)S(1)}) custom-call(s32[2]{0:T(128)S(1)} %pad_add_fusion.place, bf16[144,512]{1,0:T(8,128)(2,1)S(1)} %fusion.2.refs_0_, bf16[128,512]{1,0:T(8,128)(2,1)S(1)} %copy-done.10, bf16[144,512]{1,0:T(8,128)(2,1)S(1)} %copy-done.17, bf16[128,512]{1,0:T(8,128)(2,1)S(1)} %copy-done.29, ...), custom_call_target="tpu_custom_call" | custom-call | flops 671088640 | bytes 3932160 | tf_op jit(solution)/shard_map/pack/pallas_call | solution.py:231
  45.3 3.5 %collective-permute-done.14 = f32[2,32,512]{2,1,0:T(8,128)} collective-permute-done((f32[2,32,512]{2,1,0:T(8,128)}, f32[2,32,512]{2,1,0:T(8,128)}, u32[]{:S(2)}, u32[]{:S(2)}) %collective-permute-start.14) | collective-permute-done | bytes 131104 | tf_op jit(solution)/shard_map/ppermute | solution.py:136
  48.7 1.0 maximum_select_fusion.field
  49.8 3.0 %collective-permute-start.11 = (bf16[128,512]{1,0:T(8,128)(2,1)S(1)}, bf16[128,512]{1,0:T(8,128)(2,1)S(1)}, u32[]{:S(2)}, u32[]{:S(2)}) collective-permute-start(bf16[128,512]{1,0:T(8,128)(2,1)S(1)} %copy-done.25), channel_id=1, source_target_pairs={{0,224},{32,0},{64,32},{96,64},{128,96},{160,128},{192,160},{224,1... | collective-permute-start | bytes 393224 | tf_op jit(solution)/shard_map/ppermute | solution.py:298
  52.9 2.0 %collective-permute-start.16 = (f32[2,8,1024]{2,1,0:T(8,128)S(1)}, f32[2,8,1024]{2,1,0:T(8,128)S(1)}, u32[]{:S(2)}, u32[]{:S(2)}) collective-permute-start(f32[2,8,1024]{2,1,0:T(8,128)S(1)} %get-tuple-element.37), channel_id=1, source_target_pairs={{0,255},{1,0},{2,1},{3,2},{4,3},{5,4},{6,5},{7,6},{8,7},{9,8},{10,... | collective-permute-start | bytes 196616 | tf_op jit(solution)/shard_map/ppermute | solution.py:140
  54.9 2.6 %collective-permute-done.15.field_left = f32[2,8,1024]{2,1,0:T(8,128)S(1)} collective-permute-done((f32[2,8,1024]{2,1,0:T(8,128)S(1)}, f32[2,8,1024]{2,1,0:T(8,128)S(1)}, u32[]{:S(2)}, u32[]{:S(2)}) %collective-permute-start.15) | collective-permute-done | bytes 65568 | tf_op jit(solution)/shard_map/ppermute | solution.py:140
  57.5 3.2 %collective-permute-start.10 = (bf16[144,512]{1,0:T(8,128)(2,1)}, bf16[144,512]{1,0:T(8,128)(2,1)S(1)}, u32[]{:S(2)}, u32[]{:S(2)}) collective-permute-start(bf16[144,512]{1,0:T(8,128)(2,1)} %copy-done.14), channel_id=1, source_target_pairs={{0,224},{32,0},{64,32},{96,64},{128,96},{160,128},{192,160},{224,1... | collective-permute-start | bytes 442376 | tf_op jit(solution)/shard_map/ppermute | solution.py:298
  60.9 3.2 %collective-permute-start.13 = (bf16[128,512]{1,0:T(8,128)(2,1)S(1)}, bf16[128,512]{1,0:T(8,128)(2,1)S(1)}, u32[]{:S(2)}, u32[]{:S(2)}) collective-permute-start(bf16[128,512]{1,0:T(8,128)(2,1)S(1)} %collective-permute-done.11.refs_3_), channel_id=1, source_target_pairs={{0,224},{32,0},{64,32},{96,64},{128,96},{160,128},{192,160},{224,1... | collective-permute-start | bytes 393224 | tf_op jit(solution)/shard_map/ppermute | solution.py:298
  64.1 5.4 %collective-permute-done.9.refs_1_ = bf16[128,512]{1,0:T(8,128)(2,1)S(1)} collective-permute-done((bf16[128,512]{1,0:T(8,128)(2,1)S(1)}, bf16[128,512]{1,0:T(8,128)(2,1)S(1)}, u32[]{:S(2)}, u32[]{:S(2)}) %collective-permute-start.9) | collective-permute-done | bytes 131104 | tf_op jit(solution)/shard_map/ppermute | solution.py:298
  69.6 1.6 %pack.3 = (bf16[8,96,512]{2,1,0:T(8,128)(2,1)S(1)}, bf16[8,96,512]{2,1,0:T(8,128)(2,1)S(1)}) custom-call(s32[2]{0:T(128)S(1)} %pad_add_fusion.place, bf16[144,512]{1,0:T(8,128)(2,1)S(1)} %collective-permute-done.8.refs_0_, bf16[128,512]{1,0:T(8,128)(2,1)S(1)} %collective-permute-done.9.refs_1_, bf16[144,512]{1,0:T(8,128)(2,1)S(1)} %collective-permute-done.10.refs_2_, ...), custom_call_target="tpu_custom_call" | custom-call | flops 402653184 | bytes 2359296 | tf_op jit(solution)/shard_map/pack/pallas_call | solution.py:231
  71.1 0.9 copy-done.3
  72.0 2.3 %collective-permute-done.18.refs_3_ = bf16[8,96,512]{2,1,0:T(8,128)(2,1)S(1)} collective-permute-done((bf16[8,96,512]{2,1,0:T(8,128)(2,1)S(1)}, bf16[8,96,512]{2,1,0:T(8,128)(2,1)S(1)}, u32[]{:S(2)}, u32[]{:S(2)}) %collective-permute-start.18) | collective-permute-done | bytes 786464 | tf_op jit(solution)/shard_map/ppermute | solution.py:302
  74.3 0.9 copy-done.5
  75.2 1.1 copy-done.1
  76.3 1.3 copy-done.2
  77.6 1.1 copy-done.4
  78.7 1.1 copy-done.6
  80.5 2.1 %partial.1 = s16[8,2,128,512]{3,2,1,0:T(8,128)(2,1)S(1)} custom-call(s32[2]{0:T(128)S(1)} %copy-done.12, bf16[8,160,512]{2,1,0:T(8,128)(2,1)S(1)} %get-tuple-element.20.refs_0_, bf16[8,96,512]{2,1,0:T(8,128)(2,1)S(1)} %copy-done.4, bf16[8,160,512]{2,1,0:T(8,128)(2,1)S(1)} %copy-done.2, bf16[8,96,512]{2,1,0:T(8,128)(2,1)S(1)} %copy-done.6, ...), custom_call_target="tpu_custom_call" | custom-call | flops 1074000000 | bytes 8388608 | tf_op jit(solution)/shard_map/partial/pallas_call | solution.py:259
  82.7 35.2 %all_to_all.10 = s16[16,128,512]{2,1,0:T(8,128)(2,1)S(1)} all-to-all(s16[16,128,512]{2,1,0:T(8,128)(2,1)S(1)} %bitcast.25), channel_id=1, replica_groups=mesh['z'=8,'x'=4,'yh'=2,'c'=2,'yl'=2] {'x','yh','yl'}, dimensions={0} | all-to-all | bytes 4194304 | tf_op jit(solution)/shard_map/all_to_all | solution.py:340
  118.2 1.5 %collective-permute-start.20 = (s16[32,1024]{1,0:T(8,128)(2,1)S(1)}, s16[32,1024]{1,0:T(8,128)(2,1)S(1)}, u32[]{:S(2)}, u32[]{:S(2)}) collective-permute-start(s16[32,1024]{1,0:T(8,128)(2,1)S(1)} %fusion.8), channel_id=1, source_target_pairs={{0,255},{1,0},{2,1},{3,2},{4,3},{5,4},{6,5},{7,6},{8,7},{9,8},{10,... | collective-permute-start | bytes 196616 | tf_op jit(solution)/shard_map/ppermute | solution.py:140
  120.7 1.4 collective-permute-done.20.code_right
  122.0 2.4 %collective-permute-done.19.code_left = s16[32,1024]{1,0:T(8,128)(2,1)S(1)} collective-permute-done((s16[32,1024]{1,0:T(8,128)(2,1)S(1)}, s16[32,1024]{1,0:T(8,128)(2,1)S(1)}, u32[]{:S(2)}, u32[]{:S(2)}) %collective-permute-start.19) | collective-permute-done | bytes 65568 | tf_op jit(solution)/shard_map/ppermute | solution.py:140
  124.4 3.4 %copy-done.13 = bf16[2,2,1024,1024]{3,2,1,0:T(8,128)(2,1)S(1)} copy-done((bf16[2,2,1024,1024]{3,2,1,0:T(8,128)(2,1)S(1)}, bf16[2,2,1024,1024]{3,2,1,0:T(8,128)(2,1)}, u32[]{:S(2)}) %copy-start.13) | copy-done | bytes 8388632
  127.8 8.2 %march.1 = (f32[2,32,512]{2,1,0:T(8,128)S(1)}, bf16[2,32,512]{2,1,0:T(8,128)(2,1)S(1)}) custom-call(s32[1]{0:T(128)} %bitcast.side, s32[128,1024]{1,0:T(8,128)S(1)} %sums.1.code, s16[32,1024]{1,0:T(8,128)(2,1)S(1)} %collective-permute-done.19.code_left, s16[32,1024]{1,0:T(8,128)(2,1)S(1)} %collective-permute-done.20.code_right, ...), custom_call_target="tpu_custom_call" | custom-call | flops 3221225472 | bytes 10485760 | tf_op jit(solution)/shard_map/march/pallas_call | solution.py:114
  136.0 5.0 %collective-permute-start.21 = (bf16[2,32,512]{2,1,0:T(8,128)(2,1)S(1)}, bf16[2,32,512]{2,1,0:T(8,128)(2,1)S(1)}, u32[]{:S(2)}, u32[]{:S(2)}) collective-permute-start(bf16[2,32,512]{2,1,0:T(8,128)(2,1)S(1)} %get-tuple-element.34), channel_id=1, source_target_pairs={{0,1},{1,0},{2,3},{3,2},{4,5},{5,4},{6,7},{7,6},{8,9},{9,8},{10,11... | collective-permute-start | bytes 196616 | tf_op jit(solution)/shard_map/ppermute | solution.py:136
  140.9 2.2 %collective-permute-done.21 = bf16[2,32,512]{2,1,0:T(8,128)(2,1)S(1)} collective-permute-done((bf16[2,32,512]{2,1,0:T(8,128)(2,1)S(1)}, bf16[2,32,512]{2,1,0:T(8,128)(2,1)S(1)}, u32[]{:S(2)}, u32[]{:S(2)}) %collective-permute-start.21) | collective-permute-done | bytes 65568 | tf_op jit(solution)/shard_map/ppermute | solution.py:136
  143.2 0.9 copy.14
  (90 shorter events, 7.9 us)
Async XLA Ops:
  1.0 15.2 %copy-start.9 = (bf16[128,512]{1,0:T(8,128)(2,1)}, bf16[128,512]{1,0:T(8,128)(2,1)S(1)}, u32[]{:S(2)}) copy-start(bf16[128,512]{1,0:T(8,128)(2,1)S(1)} %get-tuple-element.41.refs_1_) | copy-start | bytes 393220
  4.1 22.2 %collective-permute-start = (bf16[144,512]{1,0:T(8,128)(2,1)S(1)}, bf16[144,512]{1,0:T(8,128)(2,1)S(1)}, u32[]{:S(2)}, u32[]{:S(2)}) collective-permute-start(bf16[144,512]{1,0:T(8,128)(2,1)S(1)} %fusion.2.refs_0_), channel_id=1, source_target_pairs={{0,32},{32,64},{64,96},{96,128},{128,160},{160,192},{192,224},{224... | collective-permute-start | bytes 442376 | tf_op jit(solution)/shard_map/ppermute | solution.py:298
  6.1 20.2 %collective-permute-start.2 = (bf16[144,512]{1,0:T(8,128)(2,1)S(1)}, bf16[144,512]{1,0:T(8,128)(2,1)S(1)}, u32[]{:S(2)}, u32[]{:S(2)}) collective-permute-start(bf16[144,512]{1,0:T(8,128)(2,1)S(1)} %fusion.2.refs_0_), channel_id=1, source_target_pairs={{0,224},{32,0},{64,32},{96,64},{128,96},{160,128},{192,160},{224,1... | collective-permute-start | bytes 442376 | tf_op jit(solution)/shard_map/ppermute | solution.py:298
  10.1 12.3 %collective-permute-start.3 = (bf16[128,512]{1,0:T(8,128)(2,1)S(1)}, bf16[128,512]{1,0:T(8,128)(2,1)S(1)}, u32[]{:S(2)}, u32[]{:S(2)}) collective-permute-start(bf16[128,512]{1,0:T(8,128)(2,1)S(1)} %get-tuple-element.41.refs_1_), channel_id=1, source_target_pairs={{0,224},{32,0},{64,32},{96,64},{128,96},{160,128},{192,160},{224,1... | collective-permute-start | bytes 393224 | tf_op jit(solution)/shard_map/ppermute | solution.py:298
  12.0 13.6 %collective-permute-start.1 = (bf16[128,512]{1,0:T(8,128)(2,1)S(1)}, bf16[128,512]{1,0:T(8,128)(2,1)S(1)}, u32[]{:S(2)}, u32[]{:S(2)}) collective-permute-start(bf16[128,512]{1,0:T(8,128)(2,1)S(1)} %get-tuple-element.41.refs_1_), channel_id=1, source_target_pairs={{0,32},{32,64},{64,96},{96,128},{128,160},{160,192},{192,224},{224... | collective-permute-start | bytes 393224 | tf_op jit(solution)/shard_map/ppermute | solution.py:298
  12.1 1.6 %copy-start = (bf16[64,4,4096]{2,1,0:T(4,128)(2,1)S(1)}, bf16[64,4,4096]{2,1,0:T(4,128)(2,1)}, u32[]{:S(2)}) copy-start(bf16[64,4,4096]{2,1,0:T(4,128)(2,1)} %weights.1) | copy-start | bytes 6291460
  16.2 6.2 %copy-start.31 = (f32[64,2,512]{2,1,0:T(2,128)S(1)}, f32[64,2,512]{2,1,0:T(2,128)}, u32[]{:S(2)}) copy-start(f32[64,2,512]{2,1,0:T(2,128)} %param.6) | copy-start | bytes 786436
  16.2 60.1 %all-to-all-start = ((bf16[8,256,512]{2,1,0:T(8,128)(2,1)}), bf16[8,256,512]{2,1,0:T(8,128)(2,1)S(1)}, u32[]{:S(2)}, u32[]{:S(2)}) async-start(bf16[8,256,512]{2,1,0:T(8,128)(2,1)} %sort.1), calls=%async_computation | async-start | bytes 4194304 | tf_op jit(solution)/shard_map/all_to_all | solution.py:319
  22.4 11.2 %copy-start.26 = (bf16[128,512]{1,0:T(8,128)(2,1)}, bf16[128,512]{1,0:T(8,128)(2,1)S(1)}, u32[]{:S(2)}) copy-start(bf16[128,512]{1,0:T(8,128)(2,1)S(1)} %collective-permute-done.3.refs_5_) | copy-start | bytes 393220
  22.4 9.4 %collective-permute-start.7 = (bf16[128,512]{1,0:T(8,128)(2,1)S(1)}, bf16[128,512]{1,0:T(8,128)(2,1)S(1)}, u32[]{:S(2)}, u32[]{:S(2)}) collective-permute-start(bf16[128,512]{1,0:T(8,128)(2,1)S(1)} %collective-permute-done.3.refs_5_), channel_id=1, source_target_pairs={{0,224},{32,0},{64,32},{96,64},{128,96},{160,128},{192,160},{224,1... | collective-permute-start | bytes 393224 | tf_op jit(solution)/shard_map/ppermute | solution.py:298
  25.6 6.8 %collective-permute-start.5 = (bf16[128,512]{1,0:T(8,128)(2,1)S(1)}, bf16[128,512]{1,0:T(8,128)(2,1)S(1)}, u32[]{:S(2)}, u32[]{:S(2)}) collective-permute-start(bf16[128,512]{1,0:T(8,128)(2,1)S(1)} %collective-permute-done.1.refs_3_), channel_id=1, source_target_pairs={{0,32},{32,64},{64,96},{96,128},{128,160},{160,192},{192,224},{224... | collective-permute-start | bytes 393224 | tf_op jit(solution)/shard_map/ppermute | solution.py:298
  26.3 7.3 %copy-start.16 = (bf16[144,512]{1,0:T(8,128)(2,1)}, bf16[144,512]{1,0:T(8,128)(2,1)S(1)}, u32[]{:S(2)}) copy-start(bf16[144,512]{1,0:T(8,128)(2,1)S(1)} %collective-permute-done.refs_2_) | copy-start | bytes 442372
  26.3 7.3 %collective-permute-start.4 = (bf16[144,512]{1,0:T(8,128)(2,1)S(1)}, bf16[144,512]{1,0:T(8,128)(2,1)S(1)}, u32[]{:S(2)}, u32[]{:S(2)}) collective-permute-start(bf16[144,512]{1,0:T(8,128)(2,1)S(1)} %collective-permute-done.refs_2_), channel_id=1, source_target_pairs={{0,32},{32,64},{64,96},{96,128},{128,160},{160,192},{192,224},{224... | collective-permute-start | bytes 442376 | tf_op jit(solution)/shard_map/ppermute | solution.py:298
  26.3 7.2 %copy-start.18 = (bf16[144,512]{1,0:T(8,128)(2,1)}, bf16[144,512]{1,0:T(8,128)(2,1)S(1)}, u32[]{:S(2)}) copy-start(bf16[144,512]{1,0:T(8,128)(2,1)S(1)} %collective-permute-done.2.refs_4_) | copy-start | bytes 442372
  26.3 7.9 %collective-permute-start.6 = (bf16[144,512]{1,0:T(8,128)(2,1)S(1)}, bf16[144,512]{1,0:T(8,128)(2,1)S(1)}, u32[]{:S(2)}, u32[]{:S(2)}) collective-permute-start(bf16[144,512]{1,0:T(8,128)(2,1)S(1)} %collective-permute-done.2.refs_4_), channel_id=1, source_target_pairs={{0,224},{32,0},{64,32},{96,64},{128,96},{160,128},{192,160},{224,1... | collective-permute-start | bytes 442376 | tf_op jit(solution)/shard_map/ppermute | solution.py:298
  30.4 18.4 %collective-permute-start.14 = (f32[2,32,512]{2,1,0:T(8,128)}, f32[2,32,512]{2,1,0:T(8,128)}, u32[]{:S(2)}, u32[]{:S(2)}) collective-permute-start(f32[2,32,512]{2,1,0:T(8,128)} %get-tuple-element.40), channel_id=1, source_target_pairs={{0,1},{1,0},{2,3},{3,2},{4,5},{5,4},{6,7},{7,6},{8,9},{9,8},{10,11... | collective-permute-start | bytes 393224 | tf_op jit(solution)/shard_map/ppermute | solution.py:136
  31.8 39.3 %copy-start.11 = (s32[2]{0:T(128)}, s32[2]{0:T(128)S(1)}, u32[]{:S(2)}) copy-start(s32[2]{0:T(128)S(1)} %pad_add_fusion.place) | copy-start | bytes 28
  34.9 0.9 copy-start.10
  35.8 0.9 copy-start.15
  36.7 0.9 copy-start.17
  37.6 0.9 copy-start.19
  38.5 0.9 copy-start.21
  39.5 0.9 copy-start.23
  40.4 0.9 copy-start.25
  41.3 0.9 copy-start.27
  42.2 0.9 copy-start.29
  43.1 5.7 %copy-start.30 = (f32[2,32,512]{2,1,0:T(8,128)S(1)}, f32[2,32,512]{2,1,0:T(8,128)}, u32[]{:S(2)}) copy-start(f32[2,32,512]{2,1,0:T(8,128)} %get-tuple-element.39) | copy-start | bytes 393220
  45.2 30.0 %collective-permute-start.17 = (bf16[8,160,512]{2,1,0:T(8,128)(2,1)S(1)}, bf16[8,160,512]{2,1,0:T(8,128)(2,1)S(1)}, u32[]{:S(2)}, u32[]{:S(2)}) collective-permute-start(bf16[8,160,512]{2,1,0:T(8,128)(2,1)S(1)} %get-tuple-element.28), channel_id=1, source_target_pairs={{0,2},{2,0},{1,3},{3,1},{4,6},{6,4},{5,7},{7,5},{8,10},{10,8},{9,1... | collective-permute-start | bytes 3932168 | tf_op jit(solution)/shard_map/ppermute | solution.py:302
  49.8 19.8 %copy-start.7 = (f32[2,32,1024]{2,1,0:T(8,128)}, f32[2,32,1024]{2,1,0:T(8,128)S(1)}, u32[]{:S(2)}) copy-start(f32[2,32,1024]{2,1,0:T(8,128)S(1)} %maximum_select_fusion.field) | copy-start | bytes 786436
  49.8 11.1 %collective-permute-start.11 = (bf16[128,512]{1,0:T(8,128)(2,1)S(1)}, bf16[128,512]{1,0:T(8,128)(2,1)S(1)}, u32[]{:S(2)}, u32[]{:S(2)}) collective-permute-start(bf16[128,512]{1,0:T(8,128)(2,1)S(1)} %copy-done.25), channel_id=1, source_target_pairs={{0,224},{32,0},{64,32},{96,64},{128,96},{160,128},{192,160},{224,1... | collective-permute-start | bytes 393224 | tf_op jit(solution)/shard_map/ppermute | solution.py:298
  52.8 8.0 %collective-permute-start.8 = (bf16[144,512]{1,0:T(8,128)(2,1)S(1)}, bf16[144,512]{1,0:T(8,128)(2,1)S(1)}, u32[]{:S(2)}, u32[]{:S(2)}) collective-permute-start(bf16[144,512]{1,0:T(8,128)(2,1)S(1)} %copy-done.21), channel_id=1, source_target_pairs={{0,32},{32,64},{64,96},{96,128},{128,160},{160,192},{192,224},{224... | collective-permute-start | bytes 442376 | tf_op jit(solution)/shard_map/ppermute | solution.py:298
  52.8 4.8 %collective-permute-start.15 = (f32[2,8,1024]{2,1,0:T(8,128)S(1)}, f32[2,8,1024]{2,1,0:T(8,128)S(1)}, u32[]{:S(2)}, u32[]{:S(2)}) collective-permute-start(f32[2,8,1024]{2,1,0:T(8,128)S(1)} %get-tuple-element.38), channel_id=1, source_target_pairs={{0,1},{1,2},{2,3},{3,4},{4,5},{5,6},{6,7},{7,8},{8,9},{9,10},{10,1... | collective-permute-start | bytes 196616 | tf_op jit(solution)/shard_map/ppermute | solution.py:140
  52.9 7.9 %collective-permute-start.16 = (f32[2,8,1024]{2,1,0:T(8,128)S(1)}, f32[2,8,1024]{2,1,0:T(8,128)S(1)}, u32[]{:S(2)}, u32[]{:S(2)}) collective-permute-start(f32[2,8,1024]{2,1,0:T(8,128)S(1)} %get-tuple-element.37), channel_id=1, source_target_pairs={{0,255},{1,0},{2,1},{3,2},{4,3},{5,4},{6,5},{7,6},{8,7},{9,8},{10,... | collective-permute-start | bytes 196616 | tf_op jit(solution)/shard_map/ppermute | solution.py:140
  57.5 12.0 %collective-permute-start.10 = (bf16[144,512]{1,0:T(8,128)(2,1)}, bf16[144,512]{1,0:T(8,128)(2,1)S(1)}, u32[]{:S(2)}, u32[]{:S(2)}) collective-permute-start(bf16[144,512]{1,0:T(8,128)(2,1)} %copy-done.14), channel_id=1, source_target_pairs={{0,224},{32,0},{64,32},{96,64},{128,96},{160,128},{192,160},{224,1... | collective-permute-start | bytes 442376 | tf_op jit(solution)/shard_map/ppermute | solution.py:298
  60.8 8.8 %collective-permute-start.12 = (bf16[144,512]{1,0:T(8,128)(2,1)S(1)}, bf16[144,512]{1,0:T(8,128)(2,1)S(1)}, u32[]{:S(2)}, u32[]{:S(2)}) collective-permute-start(bf16[144,512]{1,0:T(8,128)(2,1)S(1)} %collective-permute-done.8.refs_0_), channel_id=1, source_target_pairs={{0,32},{32,64},{64,96},{96,128},{128,160},{160,192},{192,224},{224... | collective-permute-start | bytes 442376 | tf_op jit(solution)/shard_map/ppermute | solution.py:298
  60.8 8.8 %collective-permute-start.9 = (bf16[128,512]{1,0:T(8,128)(2,1)S(1)}, bf16[128,512]{1,0:T(8,128)(2,1)S(1)}, u32[]{:S(2)}, u32[]{:S(2)}) collective-permute-start(bf16[128,512]{1,0:T(8,128)(2,1)S(1)} %copy-done.23), channel_id=1, source_target_pairs={{0,32},{32,64},{64,96},{96,128},{128,160},{160,192},{192,224},{224... | collective-permute-start | bytes 393224 | tf_op jit(solution)/shard_map/ppermute | solution.py:298
  60.9 8.7 %collective-permute-start.13 = (bf16[128,512]{1,0:T(8,128)(2,1)S(1)}, bf16[128,512]{1,0:T(8,128)(2,1)S(1)}, u32[]{:S(2)}, u32[]{:S(2)}) collective-permute-start(bf16[128,512]{1,0:T(8,128)(2,1)S(1)} %collective-permute-done.11.refs_3_), channel_id=1, source_target_pairs={{0,224},{32,0},{64,32},{96,64},{128,96},{160,128},{192,160},{224,1... | collective-permute-start | bytes 393224 | tf_op jit(solution)/shard_map/ppermute | solution.py:298
  71.1 0.9 copy-start.3
  72.0 2.3 %collective-permute-start.18 = (bf16[8,96,512]{2,1,0:T(8,128)(2,1)S(1)}, bf16[8,96,512]{2,1,0:T(8,128)(2,1)S(1)}, u32[]{:S(2)}, u32[]{:S(2)}) collective-permute-start(bf16[8,96,512]{2,1,0:T(8,128)(2,1)S(1)} %get-tuple-element.29), channel_id=1, source_target_pairs={{0,2},{2,0},{1,3},{3,1},{4,6},{6,4},{5,7},{7,5},{8,10},{10,8},{9,1... | collective-permute-start | bytes 2359304 | tf_op jit(solution)/shard_map/ppermute | solution.py:302
  75.2 1.1 copy-start.1
  76.3 1.3 copy-start.2
  77.6 1.1 copy-start.4
  78.7 1.1 copy-start.6
  118.2 6.2 %copy-start.8 = (f32[2,32,1024]{2,1,0:T(8,128)S(1)}, f32[2,32,1024]{2,1,0:T(8,128)}, u32[]{:S(2)}) copy-start(f32[2,32,1024]{2,1,0:T(8,128)} %copy-done.7) | copy-start | bytes 786436
  118.2 3.8 %collective-permute-start.20 = (s16[32,1024]{1,0:T(8,128)(2,1)S(1)}, s16[32,1024]{1,0:T(8,128)(2,1)S(1)}, u32[]{:S(2)}, u32[]{:S(2)}) collective-permute-start(s16[32,1024]{1,0:T(8,128)(2,1)S(1)} %fusion.8), channel_id=1, source_target_pairs={{0,255},{1,0},{2,1},{3,2},{4,3},{5,4},{6,5},{7,6},{8,7},{9,8},{10,... | collective-permute-start | bytes 196616 | tf_op jit(solution)/shard_map/ppermute | solution.py:140
  119.8 4.6 %collective-permute-start.19 = (s16[32,1024]{1,0:T(8,128)(2,1)S(1)}, s16[32,1024]{1,0:T(8,128)(2,1)S(1)}, u32[]{:S(2)}, u32[]{:S(2)}) collective-permute-start(s16[32,1024]{1,0:T(8,128)(2,1)S(1)} %fusion.5), channel_id=1, source_target_pairs={{0,1},{1,2},{2,3},{3,4},{4,5},{5,6},{6,7},{7,8},{8,9},{9,10},{10,1... | collective-permute-start | bytes 196616 | tf_op jit(solution)/shard_map/ppermute | solution.py:140
  124.4 3.4 %copy-start.13 = (bf16[2,2,1024,1024]{3,2,1,0:T(8,128)(2,1)S(1)}, bf16[2,2,1024,1024]{3,2,1,0:T(8,128)(2,1)}, u32[]{:S(2)}) copy-start(bf16[2,2,1024,1024]{3,2,1,0:T(8,128)(2,1)} %factors_hbm.1) | copy-start | bytes 25165828
  136.0 7.2 %collective-permute-start.21 = (bf16[2,32,512]{2,1,0:T(8,128)(2,1)S(1)}, bf16[2,32,512]{2,1,0:T(8,128)(2,1)S(1)}, u32[]{:S(2)}, u32[]{:S(2)}) collective-permute-start(bf16[2,32,512]{2,1,0:T(8,128)(2,1)S(1)} %get-tuple-element.34), channel_id=1, source_target_pairs={{0,1},{1,0},{2,3},{3,2},{4,5},{5,4},{6,7},{7,6},{8,9},{9,8},{10,11... | collective-permute-start | bytes 196616 | tf_op jit(solution)/shard_map/ppermute | solution.py:136
  (7 other events, 4.8 us)
where the time goes:
time: 145 us; the launch traced here: 144 us
  starting transfers between devices  40.9 us (28%)
  blocking collectives  35.2 us (24%)
  local copies, waits for them, and re-layouts  27.1 us (19%)
  waiting for transfers between devices  20.3 us (14%)
  Pallas kernels  16.7 us (12%)
  other arithmetic  3.63 us (3%)
    all_to_all x1, blocking collectives, per_device(): lax.all_to_all(parts.reshape(2 * PLANE, STEPS * ROWS, DEPTH), ('x', 'yh',...  35.2 us
    unnamed x67, local copies, waits for them, and re-layouts  24.9 us
    ppermute x14, starting transfers between devices, z_ring(): return lax.ppermute(value, 'z', [(i, (i + shift) % 8) for i in range(8)])  24.1 us
    pallas_call x1, Pallas kernels, march(): pl.pallas_call(march_kernel, out_shape=(jax.ShapeDtypeStruct(half, jnp.fl...  8.18 us
    ppermute x4, waiting for transfers between devices, ring_step(): lax.ppermute(value, AXES, [(i, (i + shift) % RING) for i in range(RING)])  6.37 us
    ppermute x2, starting transfers between devices, swap_dep(): return lax.ppermute(value, 'yl', [(0, 1), (1, 0)])  6.31 us
    all_to_all x1, starting transfers between devices, per_device(): lax.all_to_all(moved, ('x', 'yh'), split_axis=0, concat_axis=0, tiled=True)  6.16 us
    ppermute x14, waiting for transfers between devices, z_ring(): return lax.ppermute(value, 'z', [(i, (i + shift) % 8) for i in range(8)])  5.95 us
  transfers between devices with their start and end apart: 23, of which 8 were waited for; matrix products, arithmetic and copies ran while one was open for 1% of the time, Pallas kernels for 4%

commit v1 on v0

--- a/solution.py
+++ b/solution.py
@@ -17,12 +17,16 @@
 HALO = 8
 ROWS = 32
 EXT = ROWS + 2 * HALO
+SHARED = ROWS + HALO
 NZ = 1024
+DEPTH = NZ // 2
 STEPS = 4
 FACTORS = 2
 RING = 256
+MIB = 1024 * 1024
 VMEM = pl.BlockSpec(memory_space=pltpu.VMEM)
 SMEM = pl.BlockSpec(memory_space=pltpu.SMEM)
+ANY = pl.BlockSpec(memory_space=pl.ANY)
 
 
 def turn_code(speed):
@@ -48,16 +52,18 @@
     return first, second
 
 
-def march_kernel(
-    side, code, code_left, code_right, field, field_left, field_right, factors_hbm, keep, send, *scratch
-):
-    state, padded, rounded, codes, factors, arrived = scratch
-    copies = [pltpu.make_async_copy(factors_hbm.at[i], factors.at[i], arrived.at[i]) for i in range(FACTORS)]
-    for copy in copies:
-        copy.start()
-    state[:, 0:HALO] = field_left[...]
-    state[:, HALO : HALO + ROWS] = field[...]
-    state[:, HALO + ROWS : EXT] = field_right[...]
+def march_kernel(side, code, code_left, code_right, field, partner, near, far, factors, keep, send, *scratch):
+    state, padded, rounded, codes = scratch
+    second = side[0]
+    first = second == 0
+    rows = pl.ds(pl.multiple_of(HALO * (1 - second), HALO), SHARED)
+    outer = pl.ds(pl.multiple_of(SHARED * second, HALO), HALO)
+    here = pl.ds(pl.multiple_of(DEPTH * second, DEPTH), DEPTH)
+    there = pl.ds(pl.multiple_of(DEPTH * (1 - second), DEPTH), DEPTH)
+    state[:, rows, here] = field[:, pl.ds(pl.multiple_of((2 * ROWS - SHARED) * second, HALO), SHARED)]
+    state[:, rows, there] = partner[...]
+    state[:, outer, here] = far[...]
+    state[:, outer, there] = near[...]
     padded[:, 0:HALO] = jnp.zeros((2, HALO, NZ), jnp.float32)
     padded[:, HALO + EXT :] = jnp.zeros((2, HALO, NZ), jnp.float32)
     edge, body = STEPS * HALO, STEPS * ROWS
@@ -87,8 +93,6 @@
             padded[1, HALO : HALO + EXT] + couple_real * laplace[1] + couple_imag * laplace[0]
         ).astype(jnp.bfloat16)
         for factor in range(FACTORS):
-            if step == 0:
-                copies[factor].wait()
             left = rounded[...]
             for column in range(0, NZ, 256):
                 by_real = jnp.dot(
@@ -102,34 +106,50 @@
             if factor + 1 < FACTORS:
                 rounded[0:EXT] = state[0].astype(jnp.bfloat16)
                 rounded[EXT : 2 * EXT] = state[1].astype(jnp.bfloat16)
-    low = state[:, HALO : HALO + ROWS, 0 : NZ // 2]
-    high = state[:, HALO : HALO + ROWS, NZ // 2 :]
-    first = side[0] == 0
+    low = state[:, HALO : HALO + ROWS, 0:DEPTH]
+    high = state[:, HALO : HALO + ROWS, DEPTH:NZ]
     keep[...] = jnp.where(first, low, high)
     send[...] = jnp.where(first, high, low).astype(jnp.bfloat16)
 
 
-def march(side, code, code_left, code_right, field, field_left, field_right, factors):
-    half = (2, ROWS, NZ // 2)
+def march(side, code, code_left, code_right, field, partner, near, far, factors):
     return pl.pallas_call(
         march_kernel,
-        out_shape=(jax.ShapeDtypeStruct(half, jnp.float32), jax.ShapeDtypeStruct(half, jnp.bfloat16)),
-        in_specs=[SMEM] + [VMEM] * 6 + [pl.BlockSpec(memory_space=pl.ANY)],
+        out_shape=(
+            jax.ShapeDtypeStruct((2, ROWS, DEPTH), jnp.float32),
+            jax.ShapeDtypeStruct((2, ROWS, DEPTH), jnp.bfloat16),
+        ),
+        in_specs=[SMEM] + [VMEM] * 8,
         out_specs=(VMEM, VMEM),
         scratch_shapes=[
             pltpu.VMEM((2, EXT, NZ), jnp.float32),
             pltpu.VMEM((2, EXT + 2 * HALO, NZ), jnp.float32),
             pltpu.VMEM((2 * EXT, NZ), jnp.bfloat16),
             pltpu.VMEM((NZ // 128, STEPS * EXT, 128), jnp.int32),
-            pltpu.VMEM((FACTORS, 2, NZ, NZ), jnp.bfloat16),
-            pltpu.SemaphoreType.DMA((FACTORS,)),
         ],
-        compiler_params=pltpu.CompilerParams(vmem_limit_bytes=40 * 1024 * 1024),
+        compiler_params=pltpu.CompilerParams(vmem_limit_bytes=24 * MIB),
         cost_estimate=pl.CostEstimate(
             flops=2 * 8 * 2 * EXT * NZ * 2 * NZ, bytes_accessed=10 * 1024 * 1024, transcendentals=0
         ),
         name="march",
-    )(side, code, code_left, code_right, field, field_left, field_right, factors)
+    )(side, code, code_left, code_right, field, partner, near, far, factors)
+
+
+def merge_kernel(side, keep, other, out):
+    for part in range(2):
+        out[pl.ds(side[0] * ROWS, ROWS), part, :] = keep[part]
+        out[pl.ds((1 - side[0]) * ROWS, ROWS), part, :] = other[part].astype(jnp.float32)
+
+
+def merge(side, keep, other):
+    return pl.pallas_call(
+        merge_kernel,
+        out_shape=jax.ShapeDtypeStruct((2 * ROWS, 2, DEPTH), jnp.float32),
+        in_specs=[SMEM, VMEM, VMEM],
+        out_specs=VMEM,
+        compiler_params=pltpu.CompilerParams(vmem_limit_bytes=12 * MIB),
+        name="merge",
+    )(side, keep, other)
 
 
 def swap_dep(value):
@@ -140,27 +160,20 @@
     return lax.ppermute(value, AXES, [(i, (i + shift) % RING) for i in range(RING)])
 
 
-def own_rows_all_depths(first, value, dim, depth_dim):
-    top = lax.slice_in_dim(value, 0, ROWS, axis=dim)
-    bottom = lax.slice_in_dim(value, ROWS, 2 * ROWS, axis=dim)
-    mine = jnp.where(first, top, bottom)
-    other = swap_dep(jnp.where(first, bottom, top))
-    return jnp.where(
-        first, jnp.concatenate([mine, other], depth_dim), jnp.concatenate([other, mine], depth_dim)
-    )
-
-
-def with_halo(value, width):
-    before = ring_step(value[:, -width:], 1)
-    after = ring_step(value[:, :width], -1)
-    return before, after
+def exchange_field(first, field):
+    top, bottom = field[:, :HALO], field[:, -HALO:]
+    partner = swap_dep(jnp.where(first, field[:, -SHARED:], field[:, :SHARED]))
+    across = [(i, i + 1 if i % 2 else i - 1) for i in range(RING)]
+    near = lax.ppermute(jnp.where(first, top, bottom), AXES, [(i, j % RING) for i, j in across])
+    along = [(i, i - 2 if i % 2 else i + 2) for i in range(RING)]
+    far = lax.ppermute(jnp.where(first, bottom, top), AXES, [(i, j % RING) for i, j in along])
+    return partner, near, far
 
 
 PLANE = 8
 SLOTS = 512
 BCOL = 256
 CAP = 32
-DEPTH = NZ // 2
 EARLY = (0, -1, 1, -2, 2)
 LATE = (-3, 3, 4)
 
@@ -191,20 +204,35 @@
         grid=(2 * ROWS // block,),
         in_specs=[pl.BlockSpec((block, STEPS, 8 * SLOTS), lambda i: (i, 0, 0))],
         out_specs=pl.BlockSpec((PLANE, block * STEPS, SLOTS), lambda i: (0, i, 0)),
-        compiler_params=pltpu.CompilerParams(vmem_limit_bytes=12 * 1024 * 1024),
+        compiler_params=pltpu.CompilerParams(vmem_limit_bytes=12 * MIB),
         cost_estimate=pl.CostEstimate(flops=0, bytes_accessed=4 * 1024 * 1024, transcendentals=0),
         name="sort",
     )(weights)
 
 
 def pack_kernel(place, *refs):
-    pieces, (mine, other) = refs[:-2], refs[-2:]
+    pieces, (mine, other, held, rows, came, left) = refs[:-6], refs[-6:]
+    bricks = held.shape[0]
+    per_brick = len(pieces) // bricks
+    arrivals = []
+    for i in range(bricks):
+        start, pair = 0, []
+        for j, piece in enumerate(pieces[per_brick * i : per_brick * (i + 1)]):
+            target = held.at[i, start : start + piece.shape[0]]
+            pair.append(pltpu.make_async_copy(piece, target, came.at[i, j]))
+            start += piece.shape[0]
+        arrivals.append(pair)
+    for pair in arrivals:
+        for copy in pair:
+            copy.start()
     z, core = place[0], place[1]
     line = lax.broadcasted_iota(jnp.int32, (16, BCOL), 0)
     column = lax.broadcasted_iota(jnp.int32, (BCOL // 2, 2 * BCOL), 0)
-    for brick in range(len(pieces) // 2):
-        low, high = pieces[2 * brick], pieces[2 * brick + 1]
-        table = low[BCOL // 2 :, 0:BCOL].astype(jnp.float32)
+    departures = []
+    for brick in range(bricks):
+        for copy in arrivals[brick]:
+            copy.wait()
+        table = held[brick, 0:16, 0:BCOL].astype(jnp.float32)
         index = jnp.concatenate(
             [
                 jnp.sum(jnp.where(line == z * 2 + target, table, 0.0), axis=0, keepdims=True)
@@ -213,30 +241,42 @@
             axis=1,
         ).astype(jnp.int32)
         total = None
-        for half, ref in enumerate((low, high)):
+        for half in range(2):
             onehot = jnp.where(column + half * (BCOL // 2) == index, 1.0, 0.0).astype(jnp.bfloat16)
+            start = 16 + half * (BCOL // 2)
             part = lax.dot_general(
-                onehot, ref[0 : BCOL // 2, :], (((0,), (0,)), ((), ())), preferred_element_type=jnp.float32
+                onehot,
+                held[brick, start : start + BCOL // 2, :],
+                (((0,), (0,)), ((), ())),
+                preferred_element_type=jnp.float32,
             )
             total = part if total is None else total + part
         total = total.astype(jnp.bfloat16)
         span = slice(brick * CAP, (brick + 1) * CAP)
-        mine[:, span, :] = total[:BCOL].reshape(PLANE, CAP, DEPTH)
-        other[:, span, :] = total[BCOL:].reshape(PLANE, CAP, DEPTH)
-
-
-def pack(place, pieces):
-    bricks = len(pieces) // 2
+        for target, out in enumerate((mine, other)):
+            rows[target, :, span, :] = total[target * BCOL : (target + 1) * BCOL].reshape(PLANE, CAP, DEPTH)
+            copy = pltpu.make_async_copy(rows.at[target, :, span, :], out.at[:, span, :], left.at[brick, target])
+            copy.start()
+            departures.append(copy)
+    for copy in departures:
+        copy.wait()
+
+
+def pack(place, pieces, bricks, room):
     shape = jax.ShapeDtypeStruct((PLANE, bricks * CAP, DEPTH), jnp.bfloat16)
     return pl.pallas_call(
         pack_kernel,
         out_shape=(shape, shape),
-        in_specs=[SMEM] + [VMEM] * len(pieces),
-        out_specs=(VMEM, VMEM),
-        compiler_params=pltpu.CompilerParams(vmem_limit_bytes=12 * 1024 * 1024),
-        cost_estimate=pl.CostEstimate(
-            flops=bricks * 2 * 512 * 256 * 512, bytes_accessed=bricks * 768 * 1024, transcendentals=0
-        ),
+        in_specs=[SMEM] + [ANY] * len(pieces),
+        out_specs=(ANY, ANY),
+        scratch_shapes=[
+            pltpu.VMEM((bricks, BCOL + 16, DEPTH), jnp.bfloat16),
+            pltpu.VMEM((2, PLANE, bricks * CAP, DEPTH), jnp.bfloat16),
+            pltpu.SemaphoreType.DMA((bricks, 2)),
+            pltpu.SemaphoreType.DMA((bricks, 2)),
+        ],
+        compiler_params=pltpu.CompilerParams(vmem_limit_bytes=room),
+        cost_estimate=pl.CostEstimate(flops=bricks * 400_000_000, bytes_accessed=1024, transcendentals=0),
         name="pack",
     )(place, *pieces)
 
@@ -262,7 +302,7 @@
         in_specs=[SMEM] + [VMEM] * 5,
         out_specs=VMEM,
         scratch_shapes=[pltpu.VMEM((PLANE, SLOTS, DEPTH), jnp.bfloat16)],
-        compiler_params=pltpu.CompilerParams(vmem_limit_bytes=20 * 1024 * 1024),
+        compiler_params=pltpu.CompilerParams(vmem_limit_bytes=20 * MIB),
         cost_estimate=pl.CostEstimate(flops=2 * 537_000_000, bytes_accessed=8 * 1024 * 1024, transcendentals=0),
         name="partial",
     )(place, *groups, weights)
@@ -282,7 +322,7 @@
         out_shape=jax.ShapeDtypeStruct((STEPS * ROWS, NZ), jnp.int32),
         in_specs=[VMEM],
         out_specs=VMEM,
-        compiler_params=pltpu.CompilerParams(vmem_limit_bytes=12 * 1024 * 1024),
+        compiler_params=pltpu.CompilerParams(vmem_limit_bytes=12 * MIB),
         cost_estimate=pl.CostEstimate(flops=2_000_000, bytes_accessed=2_500_000, transcendentals=0),
         name="sums",
     )(parts)
@@ -302,54 +342,61 @@
     return lax.ppermute(value, "c", [(0, 1), (1, 0)])
 
 
-def gather_bricks(low, high):
-    pieces = {(0, 0): low, (0, 1): high}
-    for step in range(1, 4):
-        for half in range(2):
-            for way in (-1, 1):
-                pieces[way * step, half] = z_ring(pieces[way * (step - 1), half], -way)
-    pieces[4, 0] = z_ring(pieces[-3, 0], 1)
-    pieces[4, 1] = z_ring(pieces[3, 1], -1)
-    return pieces
+def first_step(brick):
+    return z_ring(brick, 1), z_ring(brick, -1)
+
+
+def gather_and_pack(place, brick, before, after):
+    whole = {0: brick, -1: before, 1: after}
+    for step in range(2, 4):
+        for way in (-1, 1):
+            whole[way * step] = z_ring(whole[way * (step - 1)], -way)
+    early = pack(place, [whole[shift] for shift in EARLY], len(EARLY), 56 * MIB)
+    early, whole[-3], whole[3] = lax.optimization_barrier((early, whole[-3], whole[3]))
+    mine_early, other_early = early
+    whole[4] = z_ring(whole[-3], 1)
+    other_early = swap_core(other_early)
+    mine_late, other_late = pack(place, [whole[shift] for shift in LATE], len(LATE), 12 * MIB)
+    other_late = swap_core(other_late)
+    return mine_early, mine_late, other_early, other_late
+
+
+def nothing_packed(place, brick, before, after):
+    rows = [jnp.zeros((PLANE, len(group) * CAP, DEPTH), brick.dtype) for group in (EARLY, LATE)]
+    return rows[0], rows[1], rows[0], rows[1]
 
 
 def per_device(field, brick_speed, send_index, send_count, weights, propagator):
-    first = lax.axis_index("yl") == 0
-    moved = sort_weights(weights)
+    slots = lax.broadcasted_iota(jnp.int32, send_index.shape, 2)
+    chosen = jnp.where(slots < send_count[:, :, None], send_index, -1).astype(jnp.bfloat16)
+    chosen = chosen.reshape(8, 8, 2, CAP).transpose(0, 2, 1, 3).reshape(16, BCOL)
+    brick = jnp.concatenate([jnp.pad(chosen, ((0, 0), (0, DEPTH - BCOL))), brick_speed])
+    place = jnp.stack([lax.axis_index("z"), lax.axis_index("c")]).astype(jnp.int32)
+    side = lax.axis_index("yl").astype(jnp.int32).reshape(1)
+    brick, place, side = lax.optimization_barrier((brick, place, side))
+    first = side[0] == 0
+
+    before, after = first_step(brick)
+    before, after, moved = lax.optimization_barrier((before, after, sort_weights(weights)))
     moved = lax.all_to_all(moved, ("x", "yh"), split_axis=0, concat_axis=0, tiled=True)
-
-    chosen = send_index[0]
-    slots = lax.broadcasted_iota(jnp.int32, chosen.shape, 1)
-    chosen = jnp.where(slots < send_count[0][:, None], chosen, -1).astype(jnp.bfloat16)
-    chosen = chosen.reshape(8, 8, 2, CAP).transpose(0, 2, 1, 3).reshape(16, BCOL)
-    chosen = jnp.pad(chosen, ((0, 0), (0, DEPTH - BCOL)))
-    low = jnp.concatenate([brick_speed[: BCOL // 2], chosen])
-    pieces = gather_bricks(low, brick_speed[BCOL // 2 :])
-    place = jnp.stack([lax.axis_index("z"), lax.axis_index("c")]).astype(jnp.int32)
-
-    own = own_rows_all_depths(first, field.transpose(1, 0, 2), 1, 2)
-    own_left, own_right = with_halo(own, HALO)
-
-    mine_early, other_early = pack(place, [pieces[shift, half] for shift in EARLY for half in range(2)])
-    other_early = swap_core(other_early)
-    late = [pieces[shift, half] for shift in LATE for half in range(2)]
-    late, own, own_left, own_right = lax.optimization_barrier((late, own, own_left, own_right))
-    mine_late, other_late = pack(place, late)
-    other_late = swap_core(other_late)
-    parts = partial_codes(place, (mine_early, mine_late, other_early, other_late), moved)
+    groups = lax.cond(
+        send_count[0, 0] <= CAP, gather_and_pack, nothing_packed, place, brick, before, after
+    )
+    parts = partial_codes(place, groups, moved)
+
+    field, parts = lax.optimization_barrier((field.transpose(1, 0, 2), parts))
+    partner, near, far = exchange_field(first, field)
     parts = lax.all_to_all(
         parts.reshape(2 * PLANE, STEPS * ROWS, DEPTH), ("x", "yh", "yl"), split_axis=0, concat_axis=0, tiled=True
     ).reshape(PLANE, 2, STEPS * ROWS, DEPTH)
+    parts, partner, near, far = lax.optimization_barrier((parts, partner, near, far))
     edge = STEPS * HALO
-    code_left = ring_step(edge_codes(parts[:, :, -edge:]), 1)
-    code_right = ring_step(edge_codes(parts[:, :, :edge]), -1)
+    edges = (edge_codes(parts[:, :, -edge:]), edge_codes(parts[:, :, :edge]))
+    code_left, code_right = ring_step(edges[0], 1), ring_step(edges[1], -1)
     code = sum_codes(parts)
 
-    side = jnp.where(first, 0, 1).astype(jnp.int32).reshape(1)
-    keep, send = march(side, code, code_left, code_right, own, own_left, own_right, propagator)
-    other = swap_dep(send).astype(jnp.float32)
-    out = jnp.where(first, jnp.concatenate([keep, other], 1), jnp.concatenate([other, keep], 1))
-    return out.transpose(1, 0, 2)
+    keep, send = march(side, code, code_left, code_right, field, partner, near, far, propagator)
+    return merge(side, keep, swap_dep(send))
 
 
 def solution(mesh):

time: 145 us -> 125 us (0.86)
  blocking collectives: 35.2 us -> 0 us
  waiting for transfers between devices: 20.3 us -> 48.8 us
  local copies, waits for them, and re-layouts: 27.1 us -> 7.31 us
  starting transfers between devices: 40.9 us -> 45.1 us
  Pallas kernels: 16.7 us -> 20.9 us
  other arithmetic: 3.63 us -> 2.13 us
    all_to_all x1 -> x0, blocking collectives: 35.2 us -> none  [per_device(): lax.all_to_all(parts.reshape(2 * PLANE, STEPS * ROWS, DEPTH), ('x', 'yh',...]
    ppermute x0 -> x2, waiting for transfers between devices: none -> 18.5 us  [the longest x1 18.4 us: exchange_field(): lax.ppermute(jnp.where(first, top, bottom), AXES, [(i, j % RING) for i, j...]
    unnamed x67 -> x12, local copies, waits for them, and re-layouts: 24.9 us -> 7.18 us
    ppermute x14 -> x7, waiting for transfers between devices: 5.95 us -> 18.3 us  [z_ring(): return lax.ppermute(value, 'z', [(i, (i + shift) % 8) for i in range(8)])]
    ppermute x14 -> x7, starting transfers between devices: 24.1 us -> 13.4 us  [z_ring(): return lax.ppermute(value, 'z', [(i, (i + shift) % 8) for i in range(8)])]
    all_to_all x0 -> x1, starting transfers between devices: none -> 8.28 us  [per_device(): lax.all_to_all(parts.reshape(2 * PLANE, STEPS * ROWS, DEPTH), ('x', 'yh',...]
    ppermute x0 -> x2, starting transfers between devices: none -> 8 us  [the longest x1 7.11 us: exchange_field(): lax.ppermute(jnp.where(first, bottom, top), AXES, [(i, j % RING) for i, j...]
    pallas_call x2, Pallas kernels: 3.66 us -> 6.33 us  [pack(): pl.pallas_call(pack_kernel, out_shape=(shape, shape), in_specs=[SMEM] + [...]
  transfers between devices with their start and end apart: 23 -> 17, of which waited for: 8 -> 11; matrix products, arithmetic and copies ran while one was open for 1% -> 0% of each run, Pallas kernels for 4% -> 7%
where the time goes in v1:
time: 125 us; the launch traced here: 124 us
  waiting for transfers between devices  48.8 us (39%)
  starting transfers between devices  45.1 us (36%)
  Pallas kernels  20.9 us (17%)
  local copies, waits for them, and re-layouts  7.31 us (6%)
  other arithmetic  2.13 us (2%)
    ppermute x1, waiting for transfers between devices, exchange_field(): lax.ppermute(jnp.where(first, top, bottom), AXES, [(i, j % RING) for i, j...  18.4 us
    ppermute x7, waiting for transfers between devices, z_ring(): return lax.ppermute(value, 'z', [(i, (i + shift) % 8) for i in range(8)])  18.3 us
    ppermute x7, starting transfers between devices, z_ring(): return lax.ppermute(value, 'z', [(i, (i + shift) % 8) for i in range(8)])  13.4 us
    all_to_all x1, starting transfers between devices, per_device(): lax.all_to_all(parts.reshape(2 * PLANE, STEPS * ROWS, DEPTH), ('x', 'yh',...  8.28 us
    pallas_call x1, Pallas kernels, march(): pl.pallas_call(march_kernel, out_shape=(jax.ShapeDtypeStruct((2, ROWS, DE...  7.53 us
    ppermute x2, starting transfers between devices, swap_dep(): return lax.ppermute(value, 'yl', [(0, 1), (1, 0)])  7.34 us
    unnamed x12, local copies, waits for them, and re-layouts  7.18 us
    ppermute x1, starting transfers between devices, exchange_field(): lax.ppermute(jnp.where(first, bottom, top), AXES, [(i, j % RING) for i, j...  7.11 us
  transfers between devices with their start and end apart: 17, of which 11 were waited for; matrix products, arithmetic and copies ran while one was open for 0% of the time, Pallas kernels for 7%

profile of v1, /device:TPU:8, one launch (start us, length us, event | category | flops | bytes accessed | tf_op | source)
XLA Modules:
  0.0 124.4 jit_solution(10657437445858727535)
XLA Ops:
  0.0 0.8 copy.11
  0.8 0.7 select_convert_fusion
  1.6 0.1 reshape.57
  1.7 0.1 pad_add_fusion.place
  1.7 1.0 fusion.1
  2.7 2.0 %collective-permute-start.7 = (bf16[272,512]{1,0:T(8,128)(2,1)S(1)}, bf16[272,512]{1,0:T(8,128)(2,1)S(1)}, u32[]{:S(2)}, u32[]{:S(2)}) collective-permute-start(bf16[272,512]{1,0:T(8,128)(2,1)S(1)} %fusion.1), channel_id=1, source_target_pairs={{0,32},{32,64},{64,96},{96,128},{128,160},{160,192},{192,224},{224... | collective-permute-start | bytes 835592 | tf_op jit(solution)/shard_map/ppermute | solution.py:338
  4.7 4.0 %collective-permute-start.8 = (bf16[272,512]{1,0:T(8,128)(2,1)S(1)}, bf16[272,512]{1,0:T(8,128)(2,1)}, u32[]{:S(2)}, u32[]{:S(2)}) collective-permute-start(bf16[272,512]{1,0:T(8,128)(2,1)S(1)} %fusion.1), channel_id=1, source_target_pairs={{0,224},{32,0},{64,32},{96,64},{128,96},{160,128},{192,160},{224,1... | collective-permute-start | bytes 835592 | tf_op jit(solution)/shard_map/ppermute | solution.py:338
  8.7 1.6 %copy-done.1 = bf16[64,4,4096]{2,1,0:T(4,128)(2,1)S(1)} copy-done((bf16[64,4,4096]{2,1,0:T(4,128)(2,1)S(1)}, bf16[64,4,4096]{2,1,0:T(4,128)(2,1)}, u32[]{:S(2)}) %copy-start.1) | copy-done | bytes 2097176
  10.3 2.5 %sort.1 = bf16[8,256,512]{2,1,0:T(8,128)(2,1)} custom-call(bf16[64,4,4096]{2,1,0:T(4,128)(2,1)S(1)} %copy-done.1), custom_call_target="tpu_custom_call" | custom-call | bytes 4194304 | tf_op jit(solution)/shard_map/sort/pallas_call | solution.py:201
  12.8 2.5 %collective-permute-done.7 = bf16[272,512]{1,0:T(8,128)(2,1)S(1)} collective-permute-done((bf16[272,512]{1,0:T(8,128)(2,1)S(1)}, bf16[272,512]{1,0:T(8,128)(2,1)S(1)}, u32[]{:S(2)}, u32[]{:S(2)}) %collective-permute-start.7) | collective-permute-done | bytes 278560 | tf_op jit(solution)/shard_map/ppermute | solution.py:338
  15.3 0.0 collective-permute-done.8
  15.3 6.0 %all-to-all-start = ((bf16[8,256,512]{2,1,0:T(8,128)(2,1)}), bf16[8,256,512]{2,1,0:T(8,128)(2,1)S(1)}, u32[]{:S(2)}, u32[]{:S(2)}) async-start(bf16[8,256,512]{2,1,0:T(8,128)(2,1)} %sort.1), calls=%async_computation | async-start | bytes 4194304 | tf_op jit(solution)/shard_map/all_to_all | solution.py:381
  21.4 0.1 copy.15
  21.5 32.1 %conditional.1 = (bf16[8,160,512]{2,1,0:T(8,128)(2,1)}, bf16[8,96,512]{2,1,0:T(8,128)(2,1)S(1)}, bf16[8,160,512]{2,1,0:T(8,128)(2,1)}, bf16[8,96,512]{2,1,0:T(8,128)(2,1)}) conditional(s32[]{:T(128)} %bitcast.7, () %tuple.19, (bf16[272,512]{1,0:T(8,128)(2,1)S(1)}, bf16[272,512]{1,0:T(8,128)(2,1)}, s32[2]{0:T(128)S(1)}, ...), branch_computations={%region_0.1_spmd, %region_1.2_spmd} | conditional | flops 3200000000 | bytes 16189808 | solution.py:382
  21.5 0.1 collective-permute-start
  21.6 3.2 %collective-permute-start.1 = (bf16[272,512]{1,0:T(8,128)(2,1)}, bf16[272,512]{1,0:T(8,128)(2,1)S(1)}, u32[]{:S(2)}, u32[]{:S(2)}) collective-permute-start(bf16[272,512]{1,0:T(8,128)(2,1)} %get-tuple-element.16.refs_2_), channel_id=1, source_target_pairs={{0,224},{32,0},{64,32},{96,64},{128,96},{160,128},{192,160},{224,1... | collective-permute-start | bytes 835592 | tf_op jit(solution)/shard_map/cond/branch_1_fun/ppermute | solution.py:338
  24.8 5.5 %collective-permute-done.refs_3_ = bf16[272,512]{1,0:T(8,128)(2,1)S(1)} collective-permute-done((bf16[272,512]{1,0:T(8,128)(2,1)S(1)}, bf16[272,512]{1,0:T(8,128)(2,1)S(1)}, u32[]{:S(2)}, u32[]{:S(2)}) %collective-permute-start) | collective-permute-done | bytes 278560 | tf_op jit(solution)/shard_map/cond/branch_1_fun/ppermute | solution.py:338
  30.3 0.0 collective-permute-start.2
  30.3 0.0 collective-permute-done.1.refs_4_
  30.4 3.2 %collective-permute-start.3 = (bf16[272,512]{1,0:T(8,128)(2,1)S(1)}, bf16[272,512]{1,0:T(8,128)(2,1)S(1)}, u32[]{:S(2)}, u32[]{:S(2)}) collective-permute-start(bf16[272,512]{1,0:T(8,128)(2,1)S(1)} %collective-permute-done.1.refs_4_), channel_id=1, source_target_pairs={{0,224},{32,0},{64,32},{96,64},{128,96},{160,128},{192,160},{224,1... | collective-permute-start | bytes 835592 | tf_op jit(solution)/shard_map/cond/branch_1_fun/ppermute | solution.py:338
  33.6 4.0 %pack.2 = (bf16[8,160,512]{2,1,0:T(8,128)(2,1)}, bf16[8,160,512]{2,1,0:T(8,128)(2,1)}) custom-call(s32[2]{0:T(128)S(1)} %get-tuple-element.13.place, bf16[272,512]{1,0:T(8,128)(2,1)S(1)} %get-tuple-element.14.refs_0_, bf16[272,512]{1,0:T(8,128)(2,1)S(1)} %get-tuple-element.15.refs_1_, bf16[272,512]{1,0:T(8,128)(2,1)} %get-tuple-element.16.refs_2_, ...), custom_call_target="tpu_custom_call" | custom-call | flops 2000000000 | bytes 1024 | tf_op jit(solution)/shard_map/cond/branch_1_fun/pack/pallas_call | solution.py:267
  37.6 0.6 collective-permute-done.2.refs_0_
  38.2 0.0 collective-permute-done.3.refs_1_
  38.2 0.8 collective-permute-start.4
  39.0 9.6 %collective-permute-done.4.refs_2_ = bf16[272,512]{1,0:T(8,128)(2,1)S(1)} collective-permute-done((bf16[272,512]{1,0:T(8,128)(2,1)S(1)}, bf16[272,512]{1,0:T(8,128)(2,1)S(1)}, u32[]{:S(2)}, u32[]{:S(2)}) %collective-permute-start.4) | collective-permute-done | bytes 278560 | tf_op jit(solution)/shard_map/cond/branch_1_fun/ppermute | solution.py:338
  48.7 2.4 %pack.3 = (bf16[8,96,512]{2,1,0:T(8,128)(2,1)S(1)}, bf16[8,96,512]{2,1,0:T(8,128)(2,1)S(1)}) custom-call(s32[2]{0:T(128)S(1)} %get-tuple-element.13.place, bf16[272,512]{1,0:T(8,128)(2,1)S(1)} %collective-permute-done.2.refs_0_, bf16[272,512]{1,0:T(8,128)(2,1)S(1)} %collective-permute-done.3.refs_1_, bf16[272,512]{1,0:T(8,128)(2,1)S(1)} %collective-permute-done.4.refs_2_), custom_call_target="tpu_custom_call" | custom-call | flops 1200000000 | bytes 1024 | tf_op jit(solution)/shard_map/cond/branch_1_fun/pack/pallas_call | solution.py:267
  51.0 0.1 collective-permute-start.6
  51.1 2.4 %collective-permute-done.6 = bf16[8,96,512]{2,1,0:T(8,128)(2,1)} collective-permute-done((bf16[8,96,512]{2,1,0:T(8,128)(2,1)S(1)}, bf16[8,96,512]{2,1,0:T(8,128)(2,1)}, u32[]{:S(2)}, u32[]{:S(2)}) %collective-permute-start.6) | collective-permute-done | bytes 786464 | tf_op jit(solution)/shard_map/cond/branch_1_fun/ppermute | solution.py:342
  53.6 3.5 %partial.1 = s16[8,2,128,512]{3,2,1,0:T(8,128)(2,1)S(1)} custom-call(s32[2]{0:T(128)S(1)} %pad_add_fusion.place, bf16[8,160,512]{2,1,0:T(8,128)(2,1)} %get-tuple-element.48.refs_0_, bf16[8,96,512]{2,1,0:T(8,128)(2,1)S(1)} %get-tuple-element.49.refs_1_, bf16[8,160,512]{2,1,0:T(8,128)(2,1)} %get-tuple-element.50.refs_2_, ...), custom_call_target="tpu_custom_call" | custom-call | flops 1074000000 | bytes 8388608 | tf_op jit(solution)/shard_map/partial/pallas_call | solution.py:299
  57.1 1.3 %copy-done = s16[8,2,128,512]{3,2,1,0:T(8,128)(2,1)} copy-done((s16[8,2,128,512]{3,2,1,0:T(8,128)(2,1)}, s16[8,2,128,512]{3,2,1,0:T(8,128)(2,1)S(1)}, u32[]{:S(2)}) %copy-start) | copy-done | bytes 2097176
  58.4 8.3 %all-to-all-start.1 = ((s16[16,128,512]{2,1,0:T(8,128)(2,1)}), s16[16,128,512]{2,1,0:T(8,128)(2,1)S(1)}, u32[]{:S(2)}, u32[]{:S(2)}) async-start(s16[16,128,512]{2,1,0:T(8,128)(2,1)} %bitcast.27), calls=%async_computation.1 | async-start | bytes 4194304 | tf_op jit(solution)/shard_map/all_to_all | solution.py:389
  66.7 0.4 collective-permute-start.9
  67.1 0.9 collective-permute-start.10
  68.0 7.1 %collective-permute-start.11 = (f32[2,8,512]{2,1,0:T(8,128)S(1)}, f32[2,8,512]{2,1,0:T(8,128)S(1)}, u32[]{:S(2)}, u32[]{:S(2)}) collective-permute-start(f32[2,8,512]{2,1,0:T(8,128)S(1)} %get-tuple-element.63), channel_id=1, source_target_pairs={{0,2},{1,255},{2,4},{3,1},{4,6},{5,3},{6,8},{7,5},{8,10},{9,7},{10... | collective-permute-start | bytes 98312 | tf_op jit(solution)/shard_map/ppermute | solution.py:169
  75.1 18.4 %collective-permute-done.10.near = f32[2,8,512]{2,1,0:T(8,128)S(1)} collective-permute-done((f32[2,8,512]{2,1,0:T(8,128)S(1)}, f32[2,8,512]{2,1,0:T(8,128)S(1)}, u32[]{:S(2)}, u32[]{:S(2)}) %collective-permute-start.10) | collective-permute-done | bytes 32800 | tf_op jit(solution)/shard_map/ppermute | solution.py:167
  93.6 0.8 collective-permute-done.9.partner
  94.4 2.2 %all-to-all-done.1 = s16[16,128,512]{2,1,0:T(8,128)(2,1)S(1)} async-done(((s16[16,128,512]{2,1,0:T(8,128)(2,1)}), s16[16,128,512]{2,1,0:T(8,128)(2,1)S(1)}, u32[]{:S(2)}, u32[]{:S(2)}) %all-to-all-start.1) | async-done | bytes 2097184 | tf_op jit(solution)/shard_map/all_to_all | solution.py:389
  96.6 0.3 convert_reduce_fusion
  97.0 1.8 %collective-permute-start.13 = (s16[32,1024]{1,0:T(8,128)(2,1)S(1)}, s16[32,1024]{1,0:T(8,128)(2,1)S(1)}, u32[]{:S(2)}, u32[]{:S(2)}) collective-permute-start(s16[32,1024]{1,0:T(8,128)(2,1)S(1)} %fusion.7), channel_id=1, source_target_pairs={{0,255},{1,0},{2,1},{3,2},{4,3},{5,4},{6,5},{7,6},{8,7},{9,8},{10,... | collective-permute-start | bytes 196616 | tf_op jit(solution)/shard_map/ppermute | solution.py:160
  98.8 0.1 collective-permute-start.12
  98.9 0.3 sums.1.code
  99.2 1.6 %collective-permute-done.13.code_right = s16[32,1024]{1,0:T(8,128)(2,1)S(1)} collective-permute-done((s16[32,1024]{1,0:T(8,128)(2,1)S(1)}, s16[32,1024]{1,0:T(8,128)(2,1)S(1)}, u32[]{:S(2)}, u32[]{:S(2)}) %collective-permute-start.13) | collective-permute-done | bytes 65568 | tf_op jit(solution)/shard_map/ppermute | solution.py:160
  100.7 2.8 %collective-permute-done.12.code_left = s16[32,1024]{1,0:T(8,128)(2,1)S(1)} collective-permute-done((s16[32,1024]{1,0:T(8,128)(2,1)S(1)}, s16[32,1024]{1,0:T(8,128)(2,1)S(1)}, u32[]{:S(2)}, u32[]{:S(2)}) %collective-permute-start.12) | collective-permute-done | bytes 65568 | tf_op jit(solution)/shard_map/ppermute | solution.py:160
  103.5 3.4 %copy-done.2 = bf16[2,2,1024,1024]{3,2,1,0:T(8,128)(2,1)S(1)} copy-done((bf16[2,2,1024,1024]{3,2,1,0:T(8,128)(2,1)S(1)}, bf16[2,2,1024,1024]{3,2,1,0:T(8,128)(2,1)}, u32[]{:S(2)}) %copy-start.2) | copy-done | bytes 8388632
  106.9 7.5 %march.1 = (f32[2,32,512]{2,1,0:T(8,128)S(1)}, bf16[2,32,512]{2,1,0:T(8,128)(2,1)S(1)}) custom-call(s32[1]{0:T(128)} %bitcast.5.side, s32[128,1024]{1,0:T(8,128)S(1)} %sums.1.code, s16[32,1024]{1,0:T(8,128)(2,1)S(1)} %collective-permute-done.12.code_left, s16[32,1024]{1,0:T(8,128)(2,1)S(1)} %collective-permute-done.13.code_right, ...), custom_call_target="tpu_custom_call" | custom-call | flops 3221225472 | bytes 10485760 | tf_op jit(solution)/shard_map/march/pallas_call | solution.py:116
  114.4 7.0 %collective-permute-start.14 = (bf16[2,32,512]{2,1,0:T(8,128)(2,1)S(1)}, bf16[2,32,512]{2,1,0:T(8,128)(2,1)S(1)}, u32[]{:S(2)}, u32[]{:S(2)}) collective-permute-start(bf16[2,32,512]{2,1,0:T(8,128)(2,1)S(1)} %get-tuple-element.60), channel_id=1, source_target_pairs={{0,1},{1,0},{2,3},{3,2},{4,5},{5,4},{6,7},{7,6},{8,9},{9,8},{10,11... | collective-permute-start | bytes 196616 | tf_op jit(solution)/shard_map/ppermute | solution.py:156
  121.4 2.2 %collective-permute-done.14.other = bf16[2,32,512]{2,1,0:T(8,128)(2,1)S(1)} collective-permute-done((bf16[2,32,512]{2,1,0:T(8,128)(2,1)S(1)}, bf16[2,32,512]{2,1,0:T(8,128)(2,1)S(1)}, u32[]{:S(2)}, u32[]{:S(2)}) %collective-permute-start.14) | collective-permute-done | bytes 65568 | tf_op jit(solution)/shard_map/ppermute | solution.py:156
  123.6 0.8 merge.1
  (21 shorter events, 0.1 us)
Async XLA Ops:
  2.7 12.6 %collective-permute-start.7 = (bf16[272,512]{1,0:T(8,128)(2,1)S(1)}, bf16[272,512]{1,0:T(8,128)(2,1)S(1)}, u32[]{:S(2)}, u32[]{:S(2)}) collective-permute-start(bf16[272,512]{1,0:T(8,128)(2,1)S(1)} %fusion.1), channel_id=1, source_target_pairs={{0,32},{32,64},{64,96},{96,128},{128,160},{160,192},{192,224},{224... | collective-permute-start | bytes 835592 | tf_op jit(solution)/shard_map/ppermute | solution.py:338
  4.7 10.6 %collective-permute-start.8 = (bf16[272,512]{1,0:T(8,128)(2,1)S(1)}, bf16[272,512]{1,0:T(8,128)(2,1)}, u32[]{:S(2)}, u32[]{:S(2)}) collective-permute-start(bf16[272,512]{1,0:T(8,128)(2,1)S(1)} %fusion.1), channel_id=1, source_target_pairs={{0,224},{32,0},{64,32},{96,64},{128,96},{160,128},{192,160},{224,1... | collective-permute-start | bytes 835592 | tf_op jit(solution)/shard_map/ppermute | solution.py:338
  8.7 1.6 %copy-start.1 = (bf16[64,4,4096]{2,1,0:T(4,128)(2,1)S(1)}, bf16[64,4,4096]{2,1,0:T(4,128)(2,1)}, u32[]{:S(2)}) copy-start(bf16[64,4,4096]{2,1,0:T(4,128)(2,1)} %weights.1) | copy-start | bytes 6291460
  12.8 8.6 %copy-start.4 = (s32[1,128]{1,0:T(1,128)S(1)}, s32[1,128]{1,0:T(1,128)}, u32[]{:S(2)}) copy-start(s32[1,128]{1,0:T(1,128)} %param.11) | copy-start | bytes 1540
  12.8 8.6 %copy-start.3 = (f32[64,2,512]{2,1,0:T(2,128)S(1)}, f32[64,2,512]{2,1,0:T(2,128)}, u32[]{:S(2)}) copy-start(f32[64,2,512]{2,1,0:T(2,128)} %param.8) | copy-start | bytes 786436
  15.3 38.2 %all-to-all-start = ((bf16[8,256,512]{2,1,0:T(8,128)(2,1)}), bf16[8,256,512]{2,1,0:T(8,128)(2,1)S(1)}, u32[]{:S(2)}, u32[]{:S(2)}) async-start(bf16[8,256,512]{2,1,0:T(8,128)(2,1)} %sort.1), calls=%async_computation | async-start | bytes 4194304 | tf_op jit(solution)/shard_map/all_to_all | solution.py:381
  21.5 8.9 %collective-permute-start = (bf16[272,512]{1,0:T(8,128)(2,1)S(1)}, bf16[272,512]{1,0:T(8,128)(2,1)S(1)}, u32[]{:S(2)}, u32[]{:S(2)}) collective-permute-start(bf16[272,512]{1,0:T(8,128)(2,1)S(1)} %get-tuple-element.15.refs_1_), channel_id=1, source_target_pairs={{0,32},{32,64},{64,96},{96,128},{128,160},{160,192},{192,224},{224... | collective-permute-start | bytes 835592 | tf_op jit(solution)/shard_map/cond/branch_1_fun/ppermute | solution.py:338
  21.6 8.8 %collective-permute-start.1 = (bf16[272,512]{1,0:T(8,128)(2,1)}, bf16[272,512]{1,0:T(8,128)(2,1)S(1)}, u32[]{:S(2)}, u32[]{:S(2)}) collective-permute-start(bf16[272,512]{1,0:T(8,128)(2,1)} %get-tuple-element.16.refs_2_), channel_id=1, source_target_pairs={{0,224},{32,0},{64,32},{96,64},{128,96},{160,128},{192,160},{224,1... | collective-permute-start | bytes 835592 | tf_op jit(solution)/shard_map/cond/branch_1_fun/ppermute | solution.py:338
  30.3 3.2 %copy-start.5 = (bf16[272,512]{1,0:T(8,128)(2,1)}, bf16[272,512]{1,0:T(8,128)(2,1)S(1)}, u32[]{:S(2)}) copy-start(bf16[272,512]{1,0:T(8,128)(2,1)S(1)} %collective-permute-done.refs_3_) | copy-start | bytes 835588 | tf_op jit(solution)/shard_map/cond
  30.3 7.9 %collective-permute-start.2 = (bf16[272,512]{1,0:T(8,128)(2,1)S(1)}, bf16[272,512]{1,0:T(8,128)(2,1)S(1)}, u32[]{:S(2)}, u32[]{:S(2)}) collective-permute-start(bf16[272,512]{1,0:T(8,128)(2,1)S(1)} %collective-permute-done.refs_3_), channel_id=1, source_target_pairs={{0,32},{32,64},{64,96},{96,128},{128,160},{160,192},{192,224},{224... | collective-permute-start | bytes 835592 | tf_op jit(solution)/shard_map/cond/branch_1_fun/ppermute | solution.py:338
  30.3 3.2 %copy-start.6 = (bf16[272,512]{1,0:T(8,128)(2,1)}, bf16[272,512]{1,0:T(8,128)(2,1)S(1)}, u32[]{:S(2)}) copy-start(bf16[272,512]{1,0:T(8,128)(2,1)S(1)} %collective-permute-done.1.refs_4_) | copy-start | bytes 835588 | tf_op jit(solution)/shard_map/cond
  30.4 7.8 %collective-permute-start.3 = (bf16[272,512]{1,0:T(8,128)(2,1)S(1)}, bf16[272,512]{1,0:T(8,128)(2,1)S(1)}, u32[]{:S(2)}, u32[]{:S(2)}) collective-permute-start(bf16[272,512]{1,0:T(8,128)(2,1)S(1)} %collective-permute-done.1.refs_4_), channel_id=1, source_target_pairs={{0,224},{32,0},{64,32},{96,64},{128,96},{160,128},{192,160},{224,1... | collective-permute-start | bytes 835592 | tf_op jit(solution)/shard_map/cond/branch_1_fun/ppermute | solution.py:338
  38.2 15.4 %collective-permute-start.5 = (bf16[8,160,512]{2,1,0:T(8,128)(2,1)}, bf16[8,160,512]{2,1,0:T(8,128)(2,1)}, u32[]{:S(2)}, u32[]{:S(2)}) collective-permute-start(bf16[8,160,512]{2,1,0:T(8,128)(2,1)} %get-tuple-element.23), channel_id=1, source_target_pairs={{0,2},{2,0},{1,3},{3,1},{4,6},{6,4},{5,7},{7,5},{8,10},{10,8},{9,1... | collective-permute-start | bytes 3932168 | tf_op jit(solution)/shard_map/cond/branch_1_fun/ppermute | solution.py:342
  38.2 10.5 %collective-permute-start.4 = (bf16[272,512]{1,0:T(8,128)(2,1)S(1)}, bf16[272,512]{1,0:T(8,128)(2,1)S(1)}, u32[]{:S(2)}, u32[]{:S(2)}) collective-permute-start(bf16[272,512]{1,0:T(8,128)(2,1)S(1)} %collective-permute-done.2.refs_0_), channel_id=1, source_target_pairs={{0,32},{32,64},{64,96},{96,128},{128,160},{160,192},{192,224},{224... | collective-permute-start | bytes 835592 | tf_op jit(solution)/shard_map/cond/branch_1_fun/ppermute | solution.py:338
  51.0 2.5 %collective-permute-start.6 = (bf16[8,96,512]{2,1,0:T(8,128)(2,1)S(1)}, bf16[8,96,512]{2,1,0:T(8,128)(2,1)}, u32[]{:S(2)}, u32[]{:S(2)}) collective-permute-start(bf16[8,96,512]{2,1,0:T(8,128)(2,1)S(1)} %get-tuple-element.24), channel_id=1, source_target_pairs={{0,2},{2,0},{1,3},{3,1},{4,6},{6,4},{5,7},{7,5},{8,10},{10,8},{9,1... | collective-permute-start | bytes 2359304 | tf_op jit(solution)/shard_map/cond/branch_1_fun/ppermute | solution.py:342
  57.1 1.3 %copy-start = (s16[8,2,128,512]{3,2,1,0:T(8,128)(2,1)}, s16[8,2,128,512]{3,2,1,0:T(8,128)(2,1)S(1)}, u32[]{:S(2)}) copy-start(s16[8,2,128,512]{3,2,1,0:T(8,128)(2,1)S(1)} %partial.1) | copy-start | bytes 6291460
  58.4 38.2 %all-to-all-start.1 = ((s16[16,128,512]{2,1,0:T(8,128)(2,1)}), s16[16,128,512]{2,1,0:T(8,128)(2,1)S(1)}, u32[]{:S(2)}, u32[]{:S(2)}) async-start(s16[16,128,512]{2,1,0:T(8,128)(2,1)} %bitcast.27), calls=%async_computation.1 | async-start | bytes 4194304 | tf_op jit(solution)/shard_map/all_to_all | solution.py:389
  66.7 27.7 %collective-permute-start.9 = (f32[2,40,512]{2,1,0:T(8,128)S(1)}, f32[2,40,512]{2,1,0:T(8,128)S(1)}, u32[]{:S(2)}, u32[]{:S(2)}) collective-permute-start(f32[2,40,512]{2,1,0:T(8,128)S(1)} %slice_select_fusion), channel_id=1, source_target_pairs={{0,1},{1,0},{2,3},{3,2},{4,5},{5,4},{6,7},{7,6},{8,9},{9,8},{10,11... | collective-permute-start | bytes 491528 | tf_op jit(solution)/shard_map/ppermute | solution.py:156
  67.1 26.5 %collective-permute-start.10 = (f32[2,8,512]{2,1,0:T(8,128)S(1)}, f32[2,8,512]{2,1,0:T(8,128)S(1)}, u32[]{:S(2)}, u32[]{:S(2)}) collective-permute-start(f32[2,8,512]{2,1,0:T(8,128)S(1)} %get-tuple-element.64), channel_id=1, source_target_pairs={{0,255},{1,2},{2,1},{3,4},{4,3},{5,6},{6,5},{7,8},{8,7},{9,10},{10... | collective-permute-start | bytes 98312 | tf_op jit(solution)/shard_map/ppermute | solution.py:167
  68.0 25.6 %collective-permute-start.11 = (f32[2,8,512]{2,1,0:T(8,128)S(1)}, f32[2,8,512]{2,1,0:T(8,128)S(1)}, u32[]{:S(2)}, u32[]{:S(2)}) collective-permute-start(f32[2,8,512]{2,1,0:T(8,128)S(1)} %get-tuple-element.63), channel_id=1, source_target_pairs={{0,2},{1,255},{2,4},{3,1},{4,6},{5,3},{6,8},{7,5},{8,10},{9,7},{10... | collective-permute-start | bytes 98312 | tf_op jit(solution)/shard_map/ppermute | solution.py:169
  97.0 3.8 %collective-permute-start.13 = (s16[32,1024]{1,0:T(8,128)(2,1)S(1)}, s16[32,1024]{1,0:T(8,128)(2,1)S(1)}, u32[]{:S(2)}, u32[]{:S(2)}) collective-permute-start(s16[32,1024]{1,0:T(8,128)(2,1)S(1)} %fusion.7), channel_id=1, source_target_pairs={{0,255},{1,0},{2,1},{3,2},{4,3},{5,4},{6,5},{7,6},{8,7},{9,8},{10,... | collective-permute-start | bytes 196616 | tf_op jit(solution)/shard_map/ppermute | solution.py:160
  98.8 4.8 %collective-permute-start.12 = (s16[32,1024]{1,0:T(8,128)(2,1)S(1)}, s16[32,1024]{1,0:T(8,128)(2,1)S(1)}, u32[]{:S(2)}, u32[]{:S(2)}) collective-permute-start(s16[32,1024]{1,0:T(8,128)(2,1)S(1)} %fusion.4), channel_id=1, source_target_pairs={{0,1},{1,2},{2,3},{3,4},{4,5},{5,6},{6,7},{7,8},{8,9},{9,10},{10,1... | collective-permute-start | bytes 196616 | tf_op jit(solution)/shard_map/ppermute | solution.py:160
  103.5 3.4 %copy-start.2 = (bf16[2,2,1024,1024]{3,2,1,0:T(8,128)(2,1)S(1)}, bf16[2,2,1024,1024]{3,2,1,0:T(8,128)(2,1)}, u32[]{:S(2)}) copy-start(bf16[2,2,1024,1024]{3,2,1,0:T(8,128)(2,1)} %factors.1) | copy-start | bytes 25165828
  114.4 9.2 %collective-permute-start.14 = (bf16[2,32,512]{2,1,0:T(8,128)(2,1)S(1)}, bf16[2,32,512]{2,1,0:T(8,128)(2,1)S(1)}, u32[]{:S(2)}, u32[]{:S(2)}) collective-permute-start(bf16[2,32,512]{2,1,0:T(8,128)(2,1)S(1)} %get-tuple-element.60), channel_id=1, source_target_pairs={{0,1},{1,0},{2,3},{3,2},{4,5},{5,4},{6,7},{7,6},{8,9},{9,8},{10,11... | collective-permute-start | bytes 196616 | tf_op jit(solution)/shard_map/ppermute | solution.py:156

commit v2 on v1

--- a/solution.py
+++ b/solution.py
@@ -346,7 +346,7 @@
     return z_ring(brick, 1), z_ring(brick, -1)
 
 
-def gather_and_pack(place, brick, before, after):
+def gather_and_pack(place, first, brick, before, after, field):
     whole = {0: brick, -1: before, 1: after}
     for step in range(2, 4):
         for way in (-1, 1):
@@ -354,16 +354,17 @@
     early = pack(place, [whole[shift] for shift in EARLY], len(EARLY), 56 * MIB)
     early, whole[-3], whole[3] = lax.optimization_barrier((early, whole[-3], whole[3]))
     mine_early, other_early = early
-    whole[4] = z_ring(whole[-3], 1)
+    whole[4], fields = lax.optimization_barrier((z_ring(whole[-3], 1), exchange_field(first, field)))
     other_early = swap_core(other_early)
     mine_late, other_late = pack(place, [whole[shift] for shift in LATE], len(LATE), 12 * MIB)
     other_late = swap_core(other_late)
-    return mine_early, mine_late, other_early, other_late
-
-
-def nothing_packed(place, brick, before, after):
+    return (mine_early, mine_late, other_early, other_late), fields
+
+
+def nothing_packed(place, first, brick, before, after, field):
     rows = [jnp.zeros((PLANE, len(group) * CAP, DEPTH), brick.dtype) for group in (EARLY, LATE)]
-    return rows[0], rows[1], rows[0], rows[1]
+    edges = [jnp.zeros((2, count, DEPTH), field.dtype) for count in (SHARED, HALO)]
+    return (rows[0], rows[1], rows[0], rows[1]), (edges[0], edges[1], edges[1])
 
 
 def per_device(field, brick_speed, send_index, send_count, weights, propagator):
@@ -379,17 +380,15 @@
     before, after = first_step(brick)
     before, after, moved = lax.optimization_barrier((before, after, sort_weights(weights)))
     moved = lax.all_to_all(moved, ("x", "yh"), split_axis=0, concat_axis=0, tiled=True)
-    groups = lax.cond(
-        send_count[0, 0] <= CAP, gather_and_pack, nothing_packed, place, brick, before, after
+    field = field.transpose(1, 0, 2)
+    groups, (partner, near, far) = lax.cond(
+        send_count[0, 0] <= CAP, gather_and_pack, nothing_packed, place, first, brick, before, after, field
     )
     parts = partial_codes(place, groups, moved)
 
-    field, parts = lax.optimization_barrier((field.transpose(1, 0, 2), parts))
-    partner, near, far = exchange_field(first, field)
     parts = lax.all_to_all(
         parts.reshape(2 * PLANE, STEPS * ROWS, DEPTH), ("x", "yh", "yl"), split_axis=0, concat_axis=0, tiled=True
     ).reshape(PLANE, 2, STEPS * ROWS, DEPTH)
-    parts, partner, near, far = lax.optimization_barrier((parts, partner, near, far))
     edge = STEPS * HALO
     edges = (edge_codes(parts[:, :, -edge:]), edge_codes(parts[:, :, :edge]))
     code_left, code_right = ring_step(edges[0], 1), ring_step(edges[1], -1)

time: 125 us -> 120 us (0.960)
  blocking collectives: 0 us -> 33.1 us
  waiting for transfers between devices: 48.8 us -> 20.6 us
  starting transfers between devices: 45.1 us -> 35.7 us
  local copies, waits for them, and re-layouts: 7.31 us -> 4.05 us
  Pallas kernels: 20.9 us -> 23.5 us
    all_to_all x0 -> x1, blocking collectives: none -> 33.1 us  [per_device(): lax.all_to_all(parts.reshape(2 * PLANE, STEPS * ROWS, DEPTH), ('x', 'yh',...]
    ppermute x1, waiting for transfers between devices: 18.4 us -> 1.85 us  [exchange_field(): lax.ppermute(jnp.where(first, top, bottom), AXES, [(i, j % RING) for i, j...]
    all_to_all x1 -> x0, starting transfers between devices: 8.28 us -> none  [per_device(): lax.all_to_all(parts.reshape(2 * PLANE, STEPS * ROWS, DEPTH), ('x', 'yh',...]
    ppermute x7, waiting for transfers between devices: 18.3 us -> 10.4 us  [z_ring(): return lax.ppermute(value, 'z', [(i, (i + shift) % 8) for i in range(8)])]
    unnamed x12 -> x22, local copies, waits for them, and re-layouts: 7.18 us -> 3.92 us
    all_to_all x1 -> x0, waiting for transfers between devices: 2.23 us -> none  [per_device(): lax.all_to_all(parts.reshape(2 * PLANE, STEPS * ROWS, DEPTH), ('x', 'yh',...]
    ppermute x2, waiting for transfers between devices: 4.36 us -> 2.13 us  [ring_step(): lax.ppermute(value, AXES, [(i, (i + shift) % RING) for i in range(RING)])]
    ppermute x1, waiting for transfers between devices: 0.01 us -> 1.59 us  [exchange_field(): lax.ppermute(jnp.where(first, bottom, top), AXES, [(i, j % RING) for i, j...]
  transfers between devices with their start and end apart: 17 -> 16, of which waited for: 11 -> 8; matrix products, arithmetic and copies ran while one was open for 0% -> 0% of each run, Pallas kernels for 7% -> 9%
where the time goes in v2:
time: 120 us; the launch traced here: 119 us
  starting transfers between devices  35.7 us (30%)
  blocking collectives  33.1 us (28%)
  Pallas kernels  23.5 us (20%)
  waiting for transfers between devices  20.6 us (17%)
  local copies, waits for them, and re-layouts  4.05 us (3%)
  other arithmetic  2.13 us (2%)
    all_to_all x1, blocking collectives, per_device(): lax.all_to_all(parts.reshape(2 * PLANE, STEPS * ROWS, DEPTH), ('x', 'yh',...  33.1 us
    ppermute x7, starting transfers between devices, z_ring(): return lax.ppermute(value, 'z', [(i, (i + shift) % 8) for i in range(8)])  12.5 us
    ppermute x7, waiting for transfers between devices, z_ring(): return lax.ppermute(value, 'z', [(i, (i + shift) % 8) for i in range(8)])  10.4 us
    pallas_call x1, Pallas kernels, march(): pl.pallas_call(march_kernel, out_shape=(jax.ShapeDtypeStruct((2, ROWS, DE...  8.67 us
    pallas_call x2, Pallas kernels, pack(): pl.pallas_call(pack_kernel, out_shape=(shape, shape), in_specs=[SMEM] + [...  7.83 us
    ppermute x2, starting transfers between devices, swap_dep(): return lax.ppermute(value, 'yl', [(0, 1), (1, 0)])  7.65 us
    ppermute x1, starting transfers between devices, exchange_field(): lax.ppermute(jnp.where(first, bottom, top), AXES, [(i, j % RING) for i, j...  7.19 us
    all_to_all x1, starting transfers between devices, per_device(): lax.all_to_all(moved, ('x', 'yh'), split_axis=0, concat_axis=0, tiled=True)  6.03 us
  transfers between devices with their start and end apart: 16, of which 8 were waited for; matrix products, arithmetic and copies ran while one was open for 0% of the time, Pallas kernels for 9%

profile of v2, /device:TPU:8, one launch (start us, length us, event | category | flops | bytes accessed | tf_op | source)
XLA Modules:
  0.0 119.4 jit_solution(15099440844223476029)
XLA Ops:
  0.0 0.8 copy.11
  0.8 0.7 select_convert_fusion
  1.6 0.1 reshape.55
  1.7 0.1 pad_add_fusion.place
  1.7 1.0 fusion.1
  2.7 5.9 %collective-permute-start.11 = (bf16[272,512]{1,0:T(8,128)(2,1)S(1)}, bf16[272,512]{1,0:T(8,128)(2,1)S(1)}, u32[]{:S(2)}, u32[]{:S(2)}) collective-permute-start(bf16[272,512]{1,0:T(8,128)(2,1)S(1)} %fusion.1), channel_id=1, source_target_pairs={{0,224},{32,0},{64,32},{96,64},{128,96},{160,128},{192,160},{224,1... | collective-permute-start | bytes 835592 | tf_op jit(solution)/shard_map/ppermute | solution.py:338
  8.7 0.0 collective-permute-start.10
  8.7 1.6 %copy-done = bf16[64,4,4096]{2,1,0:T(4,128)(2,1)S(1)} copy-done((bf16[64,4,4096]{2,1,0:T(4,128)(2,1)S(1)}, bf16[64,4,4096]{2,1,0:T(4,128)(2,1)}, u32[]{:S(2)}) %copy-start) | copy-done | bytes 2097176
  10.3 2.5 %sort.1 = bf16[8,256,512]{2,1,0:T(8,128)(2,1)} custom-call(bf16[64,4,4096]{2,1,0:T(4,128)(2,1)S(1)} %copy-done), custom_call_target="tpu_custom_call" | custom-call | bytes 4194304 | tf_op jit(solution)/shard_map/sort/pallas_call | solution.py:201
  12.7 1.8 %collective-permute-done.11 = bf16[272,512]{1,0:T(8,128)(2,1)S(1)} collective-permute-done((bf16[272,512]{1,0:T(8,128)(2,1)S(1)}, bf16[272,512]{1,0:T(8,128)(2,1)S(1)}, u32[]{:S(2)}, u32[]{:S(2)}) %collective-permute-start.11) | collective-permute-done | bytes 278560 | tf_op jit(solution)/shard_map/ppermute | solution.py:338
  14.6 3.4 %collective-permute-done.10 = bf16[272,512]{1,0:T(8,128)(2,1)S(1)} collective-permute-done((bf16[272,512]{1,0:T(8,128)(2,1)S(1)}, bf16[272,512]{1,0:T(8,128)(2,1)S(1)}, u32[]{:S(2)}, u32[]{:S(2)}) %collective-permute-start.10) | collective-permute-done | bytes 278560 | tf_op jit(solution)/shard_map/ppermute | solution.py:338
  18.0 0.7 copy-done.7
  18.7 6.0 %all-to-all-start = ((bf16[8,256,512]{2,1,0:T(8,128)(2,1)}), bf16[8,256,512]{2,1,0:T(8,128)(2,1)S(1)}, u32[]{:S(2)}, u32[]{:S(2)}) async-start(bf16[8,256,512]{2,1,0:T(8,128)(2,1)} %sort.1), calls=%async_computation | async-start | bytes 4194304 | tf_op jit(solution)/shard_map/all_to_all | solution.py:382
  24.8 0.1 copy.15
  24.9 0.0 copy-start.1
  24.9 0.7 copy-done.1
  25.6 34.3 %conditional.1 = (bf16[8,160,512]{2,1,0:T(8,128)(2,1)S(1)}, bf16[8,96,512]{2,1,0:T(8,128)(2,1)}, bf16[8,160,512]{2,1,0:T(8,128)(2,1)}, bf16[8,96,512]{2,1,0:T(8,...) conditional(s32[]{:T(128)} %bitcast.7, () %tuple.18, ...), branch_computations={%region_0.1_spmd, %region_1.2_spmd} | conditional | flops 3200057344 | bytes 17730060 | solution.py:384
  25.6 0.0 collective-permute-start
  25.6 3.2 %collective-permute-start.1 = (bf16[272,512]{1,0:T(8,128)(2,1)}, bf16[272,512]{1,0:T(8,128)(2,1)S(1)}, u32[]{:S(2)}, u32[]{:S(2)}) collective-permute-start(bf16[272,512]{1,0:T(8,128)(2,1)} %get-tuple-element.23.refs_2_), channel_id=1, source_target_pairs={{0,224},{32,0},{64,32},{96,64},{128,96},{160,128},{192,160},{224,1... | collective-permute-start | bytes 835592 | tf_op jit(solution)/shard_map/cond/branch_1_fun/ppermute | solution.py:338
  28.8 5.1 %collective-permute-done.refs_3_ = bf16[272,512]{1,0:T(8,128)(2,1)S(1)} collective-permute-done((bf16[272,512]{1,0:T(8,128)(2,1)}, bf16[272,512]{1,0:T(8,128)(2,1)S(1)}, u32[]{:S(2)}, u32[]{:S(2)}) %collective-permute-start) | collective-permute-done | bytes 278560 | tf_op jit(solution)/shard_map/cond/branch_1_fun/ppermute | solution.py:338
  34.0 3.2 %collective-permute-start.3 = (bf16[272,512]{1,0:T(8,128)(2,1)S(1)}, bf16[272,512]{1,0:T(8,128)(2,1)S(1)}, u32[]{:S(2)}, u32[]{:S(2)}) collective-permute-start(bf16[272,512]{1,0:T(8,128)(2,1)S(1)} %collective-permute-done.1.refs_4_), channel_id=1, source_target_pairs={{0,224},{32,0},{64,32},{96,64},{128,96},{160,128},{192,160},{224,1... | collective-permute-start | bytes 835592 | tf_op jit(solution)/shard_map/cond/branch_1_fun/ppermute | solution.py:338
  37.2 4.9 %pack.2 = (bf16[8,160,512]{2,1,0:T(8,128)(2,1)S(1)}, bf16[8,160,512]{2,1,0:T(8,128)(2,1)}) custom-call(s32[2]{0:T(128)S(1)} %get-tuple-element.20.place, bf16[272,512]{1,0:T(8,128)(2,1)} %get-tuple-element.21.refs_0_, bf16[272,512]{1,0:T(8,128)(2,1)} %get-tuple-element.22.refs_1_, bf16[272,512]{1,0:T(8,128)(2,1)} %get-tuple-element.23.refs_2_, ...), custom_call_target="tpu_custom_call" | custom-call | flops 2000000000 | bytes 1024 | tf_op jit(solution)/shard_map/cond/branch_1_fun/pack/pallas_call | solution.py:267
  42.1 0.0 collective-permute-done.2.refs_0_
  42.1 0.0 collective-permute-done.3.refs_1_
  42.2 0.1 collective-permute-start.4
  42.2 0.1 collective-permute-start.8
  42.4 1.4 %collective-permute-start.5 = (f32[2,40,512]{2,1,0:T(8,128)S(1)}, f32[2,40,512]{2,1,0:T(8,128)}, u32[]{:S(2)}, u32[]{:S(2)}) collective-permute-start(f32[2,40,512]{2,1,0:T(8,128)S(1)} %slice_select_fusion), channel_id=1, source_target_pairs={{0,1},{1,0},{2,3},{3,2},{4,5},{5,4},{6,7},{7,6},{8,9},{9,8},{10,11... | collective-permute-start | bytes 491528 | tf_op jit(solution)/shard_map/cond/branch_1_fun/ppermute | solution.py:156
  43.8 7.2 %collective-permute-start.7 = (f32[2,8,512]{2,1,0:T(8,128)S(1)}, f32[2,8,512]{2,1,0:T(8,128)}, u32[]{:S(2)}, u32[]{:S(2)}) collective-permute-start(f32[2,8,512]{2,1,0:T(8,128)S(1)} %get-tuple-element.70), channel_id=1, source_target_pairs={{0,2},{1,255},{2,4},{3,1},{4,6},{5,3},{6,8},{7,5},{8,10},{9,7},{10... | collective-permute-start | bytes 98312 | tf_op jit(solution)/shard_map/cond/branch_1_fun/ppermute | solution.py:169
  51.0 1.6 %collective-permute-done.7 = f32[2,8,512]{2,1,0:T(8,128)} collective-permute-done((f32[2,8,512]{2,1,0:T(8,128)S(1)}, f32[2,8,512]{2,1,0:T(8,128)}, u32[]{:S(2)}, u32[]{:S(2)}) %collective-permute-start.7) | collective-permute-done | bytes 32800 | tf_op jit(solution)/shard_map/cond/branch_1_fun/ppermute | solution.py:169
  52.6 1.8 %collective-permute-done.6 = f32[2,8,512]{2,1,0:T(8,128)} collective-permute-done((f32[2,8,512]{2,1,0:T(8,128)S(1)}, f32[2,8,512]{2,1,0:T(8,128)}, u32[]{:S(2)}, u32[]{:S(2)}) %collective-permute-start.6) | collective-permute-done | bytes 32800 | tf_op jit(solution)/shard_map/cond/branch_1_fun/ppermute | solution.py:167
  54.5 0.0 collective-permute-done.5
  54.5 0.0 collective-permute-done.4.refs_2_
  54.5 2.9 %pack.3 = (bf16[8,96,512]{2,1,0:T(8,128)(2,1)}, bf16[8,96,512]{2,1,0:T(8,128)(2,1)S(1)}) custom-call(s32[2]{0:T(128)S(1)} %get-tuple-element.20.place, bf16[272,512]{1,0:T(8,128)(2,1)S(1)} %collective-permute-done.2.refs_0_, bf16[272,512]{1,0:T(8,128)(2,1)S(1)} %collective-permute-done.3.refs_1_, bf16[272,512]{1,0:T(8,128)(2,1)S(1)} %collective-permute-done.4.refs_2_), custom_call_target="tpu_custom_call" | custom-call | flops 1200000000 | bytes 1024 | tf_op jit(solution)/shard_map/cond/branch_1_fun/pack/pallas_call | solution.py:267
  57.4 0.1 collective-permute-start.9
  57.5 2.4 %collective-permute-done.9 = bf16[8,96,512]{2,1,0:T(8,128)(2,1)} collective-permute-done((bf16[8,96,512]{2,1,0:T(8,128)(2,1)S(1)}, bf16[8,96,512]{2,1,0:T(8,128)(2,1)}, u32[]{:S(2)}, u32[]{:S(2)}) %collective-permute-start.9) | collective-permute-done | bytes 786464 | tf_op jit(solution)/shard_map/cond/branch_1_fun/ppermute | solution.py:342
  59.9 3.5 %partial.1 = s16[8,2,128,512]{3,2,1,0:T(8,128)(2,1)S(1)} custom-call(s32[2]{0:T(128)S(1)} %pad_add_fusion.place, bf16[8,160,512]{2,1,0:T(8,128)(2,1)S(1)} %get-tuple-element.58.refs_0_, bf16[8,96,512]{2,1,0:T(8,128)(2,1)} %get-tuple-element.59.refs_1_, bf16[8,160,512]{2,1,0:T(8,128)(2,1)} %get-tuple-element.60.refs_2_, ...), custom_call_target="tpu_custom_call" | custom-call | flops 1074000000 | bytes 8388608 | tf_op jit(solution)/shard_map/partial/pallas_call | solution.py:299
  63.4 0.0 slice-start.1
  63.4 33.1 %all_to_all.10 = s16[16,128,512]{2,1,0:T(8,128)(2,1)S(1)} all-to-all(s16[16,128,512]{2,1,0:T(8,128)(2,1)S(1)} %bitcast.27), channel_id=1, replica_groups=mesh['z'=8,'x'=4,'yh'=2,'c'=2,'yl'=2] {'x','yh','yl'}, dimensions={0} | all-to-all | bytes 4194304 | tf_op jit(solution)/shard_map/all_to_all | solution.py:389
  96.5 0.3 convert_reduce_fusion
  96.8 0.0 copy-start.2
  96.9 0.1 collective-permute-start.12
  97.0 2.1 %collective-permute-start.13 = (s16[32,1024]{1,0:T(8,128)(2,1)S(1)}, s16[32,1024]{1,0:T(8,128)(2,1)S(1)}, u32[]{:S(2)}, u32[]{:S(2)}) collective-permute-start(s16[32,1024]{1,0:T(8,128)(2,1)S(1)} %fusion.7), channel_id=1, source_target_pairs={{0,255},{1,0},{2,1},{3,2},{4,3},{5,4},{6,5},{7,6},{8,7},{9,8},{10,... | collective-permute-start | bytes 196616 | tf_op jit(solution)/shard_map/ppermute | solution.py:160
  99.1 0.3 sums.1.code
  99.4 2.1 %collective-permute-done.12.code_left = s16[32,1024]{1,0:T(8,128)(2,1)S(1)} collective-permute-done((s16[32,1024]{1,0:T(8,128)(2,1)S(1)}, s16[32,1024]{1,0:T(8,128)(2,1)S(1)}, u32[]{:S(2)}, u32[]{:S(2)}) %collective-permute-start.12) | collective-permute-done | bytes 65568 | tf_op jit(solution)/shard_map/ppermute | solution.py:160
  101.5 8.7 %march.1 = (f32[2,32,512]{2,1,0:T(8,128)S(1)}, bf16[2,32,512]{2,1,0:T(8,128)(2,1)S(1)}) custom-call(s32[1]{0:T(128)} %bitcast.6.side, s32[128,1024]{1,0:T(8,128)S(1)} %sums.1.code, s16[32,1024]{1,0:T(8,128)(2,1)S(1)} %collective-permute-done.12.code_left, s16[32,1024]{1,0:T(8,128)(2,1)S(1)} %collective-permute-done.13.code_right, ...), custom_call_target="tpu_custom_call" | custom-call | flops 3221225472 | bytes 10485760 | tf_op jit(solution)/shard_map/march/pallas_call | solution.py:116
  110.2 6.2 %collective-permute-start.14 = (bf16[2,32,512]{2,1,0:T(8,128)(2,1)S(1)}, bf16[2,32,512]{2,1,0:T(8,128)(2,1)S(1)}, u32[]{:S(2)}, u32[]{:S(2)}) collective-permute-start(bf16[2,32,512]{2,1,0:T(8,128)(2,1)S(1)} %get-tuple-element.67), channel_id=1, source_target_pairs={{0,1},{1,0},{2,3},{3,2},{4,5},{5,4},{6,7},{7,6},{8,9},{9,8},{10,11... | collective-permute-start | bytes 196616 | tf_op jit(solution)/shard_map/ppermute | solution.py:156
  116.4 2.2 %collective-permute-done.14.other = bf16[2,32,512]{2,1,0:T(8,128)(2,1)S(1)} collective-permute-done((bf16[2,32,512]{2,1,0:T(8,128)(2,1)S(1)}, bf16[2,32,512]{2,1,0:T(8,128)(2,1)S(1)}, u32[]{:S(2)}, u32[]{:S(2)}) %collective-permute-start.14) | collective-permute-done | bytes 65568 | tf_op jit(solution)/shard_map/ppermute | solution.py:156
  118.6 0.8 merge.1
  (31 shorter events, 0.1 us)
Async XLA Ops:
  2.7 10.0 %copy-start.3 = (bf16[272,512]{1,0:T(8,128)(2,1)}, bf16[272,512]{1,0:T(8,128)(2,1)S(1)}, u32[]{:S(2)}) copy-start(bf16[272,512]{1,0:T(8,128)(2,1)S(1)} %fusion.1) | copy-start | bytes 835588
  2.7 11.8 %collective-permute-start.11 = (bf16[272,512]{1,0:T(8,128)(2,1)S(1)}, bf16[272,512]{1,0:T(8,128)(2,1)S(1)}, u32[]{:S(2)}, u32[]{:S(2)}) collective-permute-start(bf16[272,512]{1,0:T(8,128)(2,1)S(1)} %fusion.1), channel_id=1, source_target_pairs={{0,224},{32,0},{64,32},{96,64},{128,96},{160,128},{192,160},{224,1... | collective-permute-start | bytes 835592 | tf_op jit(solution)/shard_map/ppermute | solution.py:338
  8.7 9.3 %collective-permute-start.10 = (bf16[272,512]{1,0:T(8,128)(2,1)S(1)}, bf16[272,512]{1,0:T(8,128)(2,1)S(1)}, u32[]{:S(2)}, u32[]{:S(2)}) collective-permute-start(bf16[272,512]{1,0:T(8,128)(2,1)S(1)} %fusion.1), channel_id=1, source_target_pairs={{0,32},{32,64},{64,96},{96,128},{128,160},{160,192},{192,224},{224... | collective-permute-start | bytes 835592 | tf_op jit(solution)/shard_map/ppermute | solution.py:338
  8.7 1.6 %copy-start = (bf16[64,4,4096]{2,1,0:T(4,128)(2,1)S(1)}, bf16[64,4,4096]{2,1,0:T(4,128)(2,1)}, u32[]{:S(2)}) copy-start(bf16[64,4,4096]{2,1,0:T(4,128)(2,1)} %weights.1) | copy-start | bytes 6291460
  12.7 12.0 %copy-start.5 = (s32[1,128]{1,0:T(1,128)S(1)}, s32[1,128]{1,0:T(1,128)}, u32[]{:S(2)}) copy-start(s32[1,128]{1,0:T(1,128)} %param.11) | copy-start | bytes 1540
  12.7 12.1 %copy-start.4 = (f32[64,2,512]{2,1,0:T(2,128)S(1)}, f32[64,2,512]{2,1,0:T(2,128)}, u32[]{:S(2)}) copy-start(f32[64,2,512]{2,1,0:T(2,128)} %param.8) | copy-start | bytes 786436
  14.6 3.4 %copy-start.6 = (bf16[272,512]{1,0:T(8,128)(2,1)}, bf16[272,512]{1,0:T(8,128)(2,1)S(1)}, u32[]{:S(2)}) copy-start(bf16[272,512]{1,0:T(8,128)(2,1)S(1)} %collective-permute-done.11) | copy-start | bytes 835588
  18.0 0.7 copy-start.7
  18.7 41.1 %all-to-all-start = ((bf16[8,256,512]{2,1,0:T(8,128)(2,1)}), bf16[8,256,512]{2,1,0:T(8,128)(2,1)S(1)}, u32[]{:S(2)}, u32[]{:S(2)}) async-start(bf16[8,256,512]{2,1,0:T(8,128)(2,1)} %sort.1), calls=%async_computation | async-start | bytes 4194304 | tf_op jit(solution)/shard_map/all_to_all | solution.py:382
  24.9 0.7 copy-start.1
  25.6 8.3 %collective-permute-start = (bf16[272,512]{1,0:T(8,128)(2,1)}, bf16[272,512]{1,0:T(8,128)(2,1)S(1)}, u32[]{:S(2)}, u32[]{:S(2)}) collective-permute-start(bf16[272,512]{1,0:T(8,128)(2,1)} %get-tuple-element.22.refs_1_), channel_id=1, source_target_pairs={{0,32},{32,64},{64,96},{96,128},{128,160},{160,192},{192,224},{224... | collective-permute-start | bytes 835592 | tf_op jit(solution)/shard_map/cond/branch_1_fun/ppermute | solution.py:338
  25.6 8.4 %collective-permute-start.1 = (bf16[272,512]{1,0:T(8,128)(2,1)}, bf16[272,512]{1,0:T(8,128)(2,1)S(1)}, u32[]{:S(2)}, u32[]{:S(2)}) collective-permute-start(bf16[272,512]{1,0:T(8,128)(2,1)} %get-tuple-element.23.refs_2_), channel_id=1, source_target_pairs={{0,224},{32,0},{64,32},{96,64},{128,96},{160,128},{192,160},{224,1... | collective-permute-start | bytes 835592 | tf_op jit(solution)/shard_map/cond/branch_1_fun/ppermute | solution.py:338
  33.9 3.2 %copy-start.8 = (bf16[272,512]{1,0:T(8,128)(2,1)}, bf16[272,512]{1,0:T(8,128)(2,1)S(1)}, u32[]{:S(2)}) copy-start(bf16[272,512]{1,0:T(8,128)(2,1)S(1)} %collective-permute-done.refs_3_) | copy-start | bytes 835588 | tf_op jit(solution)/shard_map/cond
  33.9 8.2 %collective-permute-start.2 = (bf16[272,512]{1,0:T(8,128)(2,1)S(1)}, bf16[272,512]{1,0:T(8,128)(2,1)S(1)}, u32[]{:S(2)}, u32[]{:S(2)}) collective-permute-start(bf16[272,512]{1,0:T(8,128)(2,1)S(1)} %collective-permute-done.refs_3_), channel_id=1, source_target_pairs={{0,32},{32,64},{64,96},{96,128},{128,160},{160,192},{192,224},{224... | collective-permute-start | bytes 835592 | tf_op jit(solution)/shard_map/cond/branch_1_fun/ppermute | solution.py:338
  33.9 3.2 %copy-start.9 = (bf16[272,512]{1,0:T(8,128)(2,1)}, bf16[272,512]{1,0:T(8,128)(2,1)S(1)}, u32[]{:S(2)}) copy-start(bf16[272,512]{1,0:T(8,128)(2,1)S(1)} %collective-permute-done.1.refs_4_) | copy-start | bytes 835588 | tf_op jit(solution)/shard_map/cond
  34.0 8.2 %collective-permute-start.3 = (bf16[272,512]{1,0:T(8,128)(2,1)S(1)}, bf16[272,512]{1,0:T(8,128)(2,1)S(1)}, u32[]{:S(2)}, u32[]{:S(2)}) collective-permute-start(bf16[272,512]{1,0:T(8,128)(2,1)S(1)} %collective-permute-done.1.refs_4_), channel_id=1, source_target_pairs={{0,224},{32,0},{64,32},{96,64},{128,96},{160,128},{192,160},{224,1... | collective-permute-start | bytes 835592 | tf_op jit(solution)/shard_map/cond/branch_1_fun/ppermute | solution.py:338
  42.2 12.3 %collective-permute-start.4 = (bf16[272,512]{1,0:T(8,128)(2,1)S(1)}, bf16[272,512]{1,0:T(8,128)(2,1)S(1)}, u32[]{:S(2)}, u32[]{:S(2)}) collective-permute-start(bf16[272,512]{1,0:T(8,128)(2,1)S(1)} %collective-permute-done.2.refs_0_), channel_id=1, source_target_pairs={{0,32},{32,64},{64,96},{96,128},{128,160},{160,192},{192,224},{224... | collective-permute-start | bytes 835592 | tf_op jit(solution)/shard_map/cond/branch_1_fun/ppermute | solution.py:338
  42.2 17.6 %collective-permute-start.8 = (bf16[8,160,512]{2,1,0:T(8,128)(2,1)}, bf16[8,160,512]{2,1,0:T(8,128)(2,1)}, u32[]{:S(2)}, u32[]{:S(2)}) collective-permute-start(bf16[8,160,512]{2,1,0:T(8,128)(2,1)} %get-tuple-element.33), channel_id=1, source_target_pairs={{0,2},{2,0},{1,3},{3,1},{4,6},{6,4},{5,7},{7,5},{8,10},{10,8},{9,1... | collective-permute-start | bytes 3932168 | tf_op jit(solution)/shard_map/cond/branch_1_fun/ppermute | solution.py:342
  42.4 12.1 %collective-permute-start.5 = (f32[2,40,512]{2,1,0:T(8,128)S(1)}, f32[2,40,512]{2,1,0:T(8,128)}, u32[]{:S(2)}, u32[]{:S(2)}) collective-permute-start(f32[2,40,512]{2,1,0:T(8,128)S(1)} %slice_select_fusion), channel_id=1, source_target_pairs={{0,1},{1,0},{2,3},{3,2},{4,5},{5,4},{6,7},{7,6},{8,9},{9,8},{10,11... | collective-permute-start | bytes 491528 | tf_op jit(solution)/shard_map/cond/branch_1_fun/ppermute | solution.py:156
  43.8 8.8 %collective-permute-start.7 = (f32[2,8,512]{2,1,0:T(8,128)S(1)}, f32[2,8,512]{2,1,0:T(8,128)}, u32[]{:S(2)}, u32[]{:S(2)}) collective-permute-start(f32[2,8,512]{2,1,0:T(8,128)S(1)} %get-tuple-element.70), channel_id=1, source_target_pairs={{0,2},{1,255},{2,4},{3,1},{4,6},{5,3},{6,8},{7,5},{8,10},{9,7},{10... | collective-permute-start | bytes 98312 | tf_op jit(solution)/shard_map/cond/branch_1_fun/ppermute | solution.py:169
  51.0 3.4 %collective-permute-start.6 = (f32[2,8,512]{2,1,0:T(8,128)S(1)}, f32[2,8,512]{2,1,0:T(8,128)}, u32[]{:S(2)}, u32[]{:S(2)}) collective-permute-start(f32[2,8,512]{2,1,0:T(8,128)S(1)} %get-tuple-element.71), channel_id=1, source_target_pairs={{0,255},{1,2},{2,1},{3,4},{4,3},{5,6},{6,5},{7,8},{8,7},{9,10},{10... | collective-permute-start | bytes 98312 | tf_op jit(solution)/shard_map/cond/branch_1_fun/ppermute | solution.py:167
  57.4 2.5 %collective-permute-start.9 = (bf16[8,96,512]{2,1,0:T(8,128)(2,1)S(1)}, bf16[8,96,512]{2,1,0:T(8,128)(2,1)}, u32[]{:S(2)}, u32[]{:S(2)}) collective-permute-start(bf16[8,96,512]{2,1,0:T(8,128)(2,1)S(1)} %get-tuple-element.34), channel_id=1, source_target_pairs={{0,2},{2,0},{1,3},{3,1},{4,6},{6,4},{5,7},{7,5},{8,10},{10,8},{9,1... | collective-permute-start | bytes 2359304 | tf_op jit(solution)/shard_map/cond/branch_1_fun/ppermute | solution.py:342
  59.9 41.6 %slice-start = ((s8[8388608]{0:T(1024)(128)(4,1)}), s8[4194304]{0:T(1024)(128)(4,1)S(1)}, s32[]{:S(2)}) async-start(s8[8388608]{0:T(1024)(128)(4,1)} %bitcast.28), calls=%async_computation.2 | async-start | bytes 8388608
  63.4 38.1 %slice-start.1 = ((s8[8388608]{0:T(1024)(128)(4,1)}), s8[4194304]{0:T(1024)(128)(4,1)S(1)}, s32[]{:S(2)}) async-start(s8[8388608]{0:T(1024)(128)(4,1)} %bitcast.28), calls=%async_computation.3 | async-start | bytes 8388608
  96.8 4.7 %copy-start.2 = (f32[64,2,512]{2,0,1:T(8,128)S(1)}, f32[64,2,512]{2,0,1:T(8,128)}, u32[]{:S(2)}) copy-start(f32[64,2,512]{2,0,1:T(8,128)} %copy-done.1) | copy-start | bytes 786436
  96.9 4.6 %collective-permute-start.12 = (s16[32,1024]{1,0:T(8,128)(2,1)S(1)}, s16[32,1024]{1,0:T(8,128)(2,1)S(1)}, u32[]{:S(2)}, u32[]{:S(2)}) collective-permute-start(s16[32,1024]{1,0:T(8,128)(2,1)S(1)} %fusion.4), channel_id=1, source_target_pairs={{0,1},{1,2},{2,3},{3,4},{4,5},{5,6},{6,7},{7,8},{8,9},{9,10},{10,1... | collective-permute-start | bytes 196616 | tf_op jit(solution)/shard_map/ppermute | solution.py:160
  97.0 4.5 %collective-permute-start.13 = (s16[32,1024]{1,0:T(8,128)(2,1)S(1)}, s16[32,1024]{1,0:T(8,128)(2,1)S(1)}, u32[]{:S(2)}, u32[]{:S(2)}) collective-permute-start(s16[32,1024]{1,0:T(8,128)(2,1)S(1)} %fusion.7), channel_id=1, source_target_pairs={{0,255},{1,0},{2,1},{3,2},{4,3},{5,4},{6,5},{7,6},{8,7},{9,8},{10,... | collective-permute-start | bytes 196616 | tf_op jit(solution)/shard_map/ppermute | solution.py:160
  110.2 8.4 %collective-permute-start.14 = (bf16[2,32,512]{2,1,0:T(8,128)(2,1)S(1)}, bf16[2,32,512]{2,1,0:T(8,128)(2,1)S(1)}, u32[]{:S(2)}, u32[]{:S(2)}) collective-permute-start(bf16[2,32,512]{2,1,0:T(8,128)(2,1)S(1)} %get-tuple-element.67), channel_id=1, source_target_pairs={{0,1},{1,0},{2,3},{3,2},{4,5},{5,4},{6,7},{7,6},{8,9},{9,8},{10,11... | collective-permute-start | bytes 196616 | tf_op jit(solution)/shard_map/ppermute | solution.py:156

commit v3 on v2

--- a/solution.py
+++ b/solution.py
@@ -211,28 +211,12 @@
 
 
 def pack_kernel(place, *refs):
-    pieces, (mine, other, held, rows, came, left) = refs[:-6], refs[-6:]
-    bricks = held.shape[0]
-    per_brick = len(pieces) // bricks
-    arrivals = []
-    for i in range(bricks):
-        start, pair = 0, []
-        for j, piece in enumerate(pieces[per_brick * i : per_brick * (i + 1)]):
-            target = held.at[i, start : start + piece.shape[0]]
-            pair.append(pltpu.make_async_copy(piece, target, came.at[i, j]))
-            start += piece.shape[0]
-        arrivals.append(pair)
-    for pair in arrivals:
-        for copy in pair:
-            copy.start()
+    bricks, outs = refs[:-2], refs[-2:]
     z, core = place[0], place[1]
     line = lax.broadcasted_iota(jnp.int32, (16, BCOL), 0)
     column = lax.broadcasted_iota(jnp.int32, (BCOL // 2, 2 * BCOL), 0)
-    departures = []
-    for brick in range(bricks):
-        for copy in arrivals[brick]:
-            copy.wait()
-        table = held[brick, 0:16, 0:BCOL].astype(jnp.float32)
+    for brick, held in enumerate(bricks):
+        table = held[0:16, 0:BCOL].astype(jnp.float32)
         index = jnp.concatenate(
             [
                 jnp.sum(jnp.where(line == z * 2 + target, table, 0.0), axis=0, keepdims=True)
@@ -245,40 +229,26 @@
             onehot = jnp.where(column + half * (BCOL // 2) == index, 1.0, 0.0).astype(jnp.bfloat16)
             start = 16 + half * (BCOL // 2)
             part = lax.dot_general(
-                onehot,
-                held[brick, start : start + BCOL // 2, :],
-                (((0,), (0,)), ((), ())),
-                preferred_element_type=jnp.float32,
+                onehot, held[start : start + BCOL // 2, :], (((0,), (0,)), ((), ())), preferred_element_type=jnp.float32
             )
             total = part if total is None else total + part
         total = total.astype(jnp.bfloat16)
-        span = slice(brick * CAP, (brick + 1) * CAP)
-        for target, out in enumerate((mine, other)):
-            rows[target, :, span, :] = total[target * BCOL : (target + 1) * BCOL].reshape(PLANE, CAP, DEPTH)
-            copy = pltpu.make_async_copy(rows.at[target, :, span, :], out.at[:, span, :], left.at[brick, target])
-            copy.start()
-            departures.append(copy)
-    for copy in departures:
-        copy.wait()
-
-
-def pack(place, pieces, bricks, room):
-    shape = jax.ShapeDtypeStruct((PLANE, bricks * CAP, DEPTH), jnp.bfloat16)
+        for target, out in enumerate(outs):
+            rows = total[target * BCOL : (target + 1) * BCOL].reshape(PLANE, CAP, DEPTH)
+            out[:, brick * CAP : (brick + 1) * CAP, :] = rows
+
+
+def pack(place, bricks):
+    shape = jax.ShapeDtypeStruct((PLANE, len(bricks) * CAP, DEPTH), jnp.bfloat16)
     return pl.pallas_call(
         pack_kernel,
         out_shape=(shape, shape),
-        in_specs=[SMEM] + [ANY] * len(pieces),
-        out_specs=(ANY, ANY),
-        scratch_shapes=[
-            pltpu.VMEM((bricks, BCOL + 16, DEPTH), jnp.bfloat16),
-            pltpu.VMEM((2, PLANE, bricks * CAP, DEPTH), jnp.bfloat16),
-            pltpu.SemaphoreType.DMA((bricks, 2)),
-            pltpu.SemaphoreType.DMA((bricks, 2)),
-        ],
-        compiler_params=pltpu.CompilerParams(vmem_limit_bytes=room),
-        cost_estimate=pl.CostEstimate(flops=bricks * 400_000_000, bytes_accessed=1024, transcendentals=0),
+        in_specs=[SMEM] + [VMEM] * len(bricks),
+        out_specs=(VMEM, VMEM),
+        compiler_params=pltpu.CompilerParams(vmem_limit_bytes=12 * MIB),
+        cost_estimate=pl.CostEstimate(flops=len(bricks) * 400_000_000, bytes_accessed=1024, transcendentals=0),
         name="pack",
-    )(place, *pieces)
+    )(place, *bricks)
 
 
 def partial_kernel(place, *refs):
@@ -351,12 +321,12 @@
     for step in range(2, 4):
         for way in (-1, 1):
             whole[way * step] = z_ring(whole[way * (step - 1)], -way)
-    early = pack(place, [whole[shift] for shift in EARLY], len(EARLY), 56 * MIB)
+    early = pack(place, [whole[shift] for shift in EARLY])
     early, whole[-3], whole[3] = lax.optimization_barrier((early, whole[-3], whole[3]))
     mine_early, other_early = early
     whole[4], fields = lax.optimization_barrier((z_ring(whole[-3], 1), exchange_field(first, field)))
     other_early = swap_core(other_early)
-    mine_late, other_late = pack(place, [whole[shift] for shift in LATE], len(LATE), 12 * MIB)
+    mine_late, other_late = pack(place, [whole[shift] for shift in LATE])
     other_late = swap_core(other_late)
     return (mine_early, mine_late, other_early, other_late), fields
 

time: 120 us -> 119 us (level)
  Pallas kernels: 23.5 us -> 20.8 us
  waiting for transfers between devices: 20.6 us -> 22.4 us
    pallas_call x2, Pallas kernels: 7.83 us -> 5.06 us  [pack(): pl.pallas_call(pack_kernel, out_shape=(shape, shape), in_specs=[SMEM] + [...]
    ppermute x7, waiting for transfers between devices: 10.4 us -> 12.2 us  [z_ring(): return lax.ppermute(value, 'z', [(i, (i + shift) % 8) for i in range(8)])]
  transfers between devices with their start and end apart: 16 -> 16, of which waited for: 8 -> 9; matrix products, arithmetic and copies ran while one was open for 0% -> 0% of each run, Pallas kernels for 9% -> 7%
where the time goes in v3:
time: 119 us
  starting transfers between devices  35.6 us (30%)
  blocking collectives  33.7 us (28%)
  waiting for transfers between devices  22.4 us (19%)
  Pallas kernels  20.8 us (17%)
  local copies, waits for them, and re-layouts  4.03 us (3%)
  other arithmetic  2.13 us (2%)
    all_to_all x1, blocking collectives, per_device(): lax.all_to_all(parts.reshape(2 * PLANE, STEPS * ROWS, DEPTH), ('x', 'yh',...  33.7 us
    ppermute x7, starting transfers between devices, z_ring(): return lax.ppermute(value, 'z', [(i, (i + shift) % 8) for i in range(8)])  12.4 us
    ppermute x7, waiting for transfers between devices, z_ring(): return lax.ppermute(value, 'z', [(i, (i + shift) % 8) for i in range(8)])  12.2 us
    pallas_call x1, Pallas kernels, march(): pl.pallas_call(march_kernel, out_shape=(jax.ShapeDtypeStruct((2, ROWS, DE...  8.67 us
    ppermute x2, starting transfers between devices, swap_dep(): return lax.ppermute(value, 'yl', [(0, 1), (1, 0)])  7.64 us
    ppermute x1, starting transfers between devices, exchange_field(): lax.ppermute(jnp.where(first, bottom, top), AXES, [(i, j % RING) for i, j...  7.32 us
    all_to_all x1, starting transfers between devices, per_device(): lax.all_to_all(moved, ('x', 'yh'), split_axis=0, concat_axis=0, tiled=True)  6.03 us
    pallas_call x2, Pallas kernels, pack(): pl.pallas_call(pack_kernel, out_shape=(shape, shape), in_specs=[SMEM] + [...  5.06 us
  transfers between devices with their start and end apart: 16, of which 9 were waited for; matrix products, arithmetic and copies ran while one was open for 0% of the time, Pallas kernels for 7%

profile of v3, /device:TPU:8, one launch (start us, length us, event | category | flops | bytes accessed | tf_op | source)
XLA Modules:
  0.0 118.8 jit_solution(17329710595539921650)
XLA Ops:
  0.0 0.8 copy.11
  0.8 0.7 select_convert_fusion
  1.6 0.1 reshape.55
  1.7 0.1 pad_add_fusion.place
  1.7 1.0 fusion.1
  2.7 5.9 %collective-permute-start.11 = (bf16[272,512]{1,0:T(8,128)(2,1)S(1)}, bf16[272,512]{1,0:T(8,128)(2,1)S(1)}, u32[]{:S(2)}, u32[]{:S(2)}) collective-permute-start(bf16[272,512]{1,0:T(8,128)(2,1)S(1)} %fusion.1), channel_id=1, source_target_pairs={{0,224},{32,0},{64,32},{96,64},{128,96},{160,128},{192,160},{224,1... | collective-permute-start | bytes 835592 | tf_op jit(solution)/shard_map/ppermute | solution.py:308
  8.7 0.0 collective-permute-start.10
  8.7 1.6 %copy-done = bf16[64,4,4096]{2,1,0:T(4,128)(2,1)S(1)} copy-done((bf16[64,4,4096]{2,1,0:T(4,128)(2,1)S(1)}, bf16[64,4,4096]{2,1,0:T(4,128)(2,1)}, u32[]{:S(2)}) %copy-start) | copy-done | bytes 2097176
  10.3 2.5 %sort.1 = bf16[8,256,512]{2,1,0:T(8,128)(2,1)} custom-call(bf16[64,4,4096]{2,1,0:T(4,128)(2,1)S(1)} %copy-done), custom_call_target="tpu_custom_call" | custom-call | bytes 4194304 | tf_op jit(solution)/shard_map/sort/pallas_call | solution.py:201
  12.8 1.8 %collective-permute-done.11 = bf16[272,512]{1,0:T(8,128)(2,1)S(1)} collective-permute-done((bf16[272,512]{1,0:T(8,128)(2,1)S(1)}, bf16[272,512]{1,0:T(8,128)(2,1)S(1)}, u32[]{:S(2)}, u32[]{:S(2)}) %collective-permute-start.11) | collective-permute-done | bytes 278560 | tf_op jit(solution)/shard_map/ppermute | solution.py:308
  14.6 3.4 %collective-permute-done.10 = bf16[272,512]{1,0:T(8,128)(2,1)S(1)} collective-permute-done((bf16[272,512]{1,0:T(8,128)(2,1)S(1)}, bf16[272,512]{1,0:T(8,128)(2,1)S(1)}, u32[]{:S(2)}, u32[]{:S(2)}) %collective-permute-start.10) | collective-permute-done | bytes 278560 | tf_op jit(solution)/shard_map/ppermute | solution.py:308
  18.0 0.7 copy-done.7
  18.7 6.0 %all-to-all-start = ((bf16[8,256,512]{2,1,0:T(8,128)(2,1)}), bf16[8,256,512]{2,1,0:T(8,128)(2,1)S(1)}, u32[]{:S(2)}, u32[]{:S(2)}) async-start(bf16[8,256,512]{2,1,0:T(8,128)(2,1)} %sort.1), calls=%async_computation | async-start | bytes 4194304 | tf_op jit(solution)/shard_map/all_to_all | solution.py:352
  24.8 0.1 copy.15
  24.9 0.0 copy-start.1
  24.9 0.7 copy-done.1
  25.6 33.2 %conditional.1 = (bf16[8,160,512]{2,1,0:T(8,128)(2,1)S(1)}, bf16[8,96,512]{2,1,0:T(8,128)(2,1)}, bf16[8,160,512]{2,1,0:T(8,128)(2,1)}, bf16[8,96,512]{2,1,0:T(8,...) conditional(s32[]{:T(128)} %bitcast.7, () %tuple.18, ...), branch_computations={%region_0.1_spmd, %region_1.2_spmd} | conditional | flops 3200057344 | bytes 15501779 | solution.py:354
  25.6 0.0 collective-permute-start
  25.6 3.2 %collective-permute-start.1 = (bf16[272,512]{1,0:T(8,128)(2,1)}, bf16[272,512]{1,0:T(8,128)(2,1)S(1)}, u32[]{:S(2)}, u32[]{:S(2)}) collective-permute-start(bf16[272,512]{1,0:T(8,128)(2,1)} %get-tuple-element.23.refs_2_), channel_id=1, source_target_pairs={{0,224},{32,0},{64,32},{96,64},{128,96},{160,128},{192,160},{224,1... | collective-permute-start | bytes 835592 | tf_op jit(solution)/shard_map/cond/branch_1_fun/ppermute | solution.py:308
  28.8 5.1 %collective-permute-done.refs_3_ = bf16[272,512]{1,0:T(8,128)(2,1)S(1)} collective-permute-done((bf16[272,512]{1,0:T(8,128)(2,1)}, bf16[272,512]{1,0:T(8,128)(2,1)S(1)}, u32[]{:S(2)}, u32[]{:S(2)}) %collective-permute-start) | collective-permute-done | bytes 278560 | tf_op jit(solution)/shard_map/cond/branch_1_fun/ppermute | solution.py:308
  33.9 0.0 collective-permute-start.2
  33.9 0.0 collective-permute-done.1.refs_4_
  33.9 3.2 %collective-permute-start.3 = (bf16[272,512]{1,0:T(8,128)(2,1)S(1)}, bf16[272,512]{1,0:T(8,128)(2,1)S(1)}, u32[]{:S(2)}, u32[]{:S(2)}) collective-permute-start(bf16[272,512]{1,0:T(8,128)(2,1)S(1)} %collective-permute-done.1.refs_4_), channel_id=1, source_target_pairs={{0,224},{32,0},{64,32},{96,64},{128,96},{160,128},{192,160},{224,1... | collective-permute-start | bytes 835592 | tf_op jit(solution)/shard_map/cond/branch_1_fun/ppermute | solution.py:308
  37.2 2.7 %pack.2 = (bf16[8,160,512]{2,1,0:T(8,128)(2,1)S(1)}, bf16[8,160,512]{2,1,0:T(8,128)(2,1)S(1)}) custom-call(s32[2]{0:T(128)S(1)} %get-tuple-element.20.place, bf16[272,512]{1,0:T(8,128)(2,1)} %get-tuple-element.21.refs_0_, bf16[272,512]{1,0:T(8,128)(2,1)} %get-tuple-element.22.refs_1_, bf16[272,512]{1,0:T(8,128)(2,1)} %get-tuple-element.23.refs_2_, ...), custom_call_target="tpu_custom_call" | custom-call | flops 2000000000 | bytes 1024 | tf_op jit(solution)/shard_map/cond/branch_1_fun/pack/pallas_call | solution.py:243
  39.9 1.8 %collective-permute-done.2.refs_0_ = bf16[272,512]{1,0:T(8,128)(2,1)S(1)} collective-permute-done((bf16[272,512]{1,0:T(8,128)(2,1)S(1)}, bf16[272,512]{1,0:T(8,128)(2,1)S(1)}, u32[]{:S(2)}, u32[]{:S(2)}) %collective-permute-start.2) | collective-permute-done | bytes 278560 | tf_op jit(solution)/shard_map/cond/branch_1_fun/ppermute | solution.py:308
  41.7 1.4 %collective-permute-start.5 = (f32[2,40,512]{2,1,0:T(8,128)S(1)}, f32[2,40,512]{2,1,0:T(8,128)}, u32[]{:S(2)}, u32[]{:S(2)}) collective-permute-start(f32[2,40,512]{2,1,0:T(8,128)S(1)} %slice_select_fusion), channel_id=1, source_target_pairs={{0,1},{1,0},{2,3},{3,2},{4,5},{5,4},{6,7},{7,6},{8,9},{9,8},{10,11... | collective-permute-start | bytes 491528 | tf_op jit(solution)/shard_map/cond/branch_1_fun/ppermute | solution.py:156
  43.2 7.3 %collective-permute-start.7 = (f32[2,8,512]{2,1,0:T(8,128)S(1)}, f32[2,8,512]{2,1,0:T(8,128)}, u32[]{:S(2)}, u32[]{:S(2)}) collective-permute-start(f32[2,8,512]{2,1,0:T(8,128)S(1)} %get-tuple-element.70), channel_id=1, source_target_pairs={{0,2},{1,255},{2,4},{3,1},{4,6},{5,3},{6,8},{7,5},{8,10},{9,7},{10... | collective-permute-start | bytes 98312 | tf_op jit(solution)/shard_map/cond/branch_1_fun/ppermute | solution.py:169
  50.5 0.0 collective-permute-start.6
  50.5 1.6 %collective-permute-done.7 = f32[2,8,512]{2,1,0:T(8,128)} collective-permute-done((f32[2,8,512]{2,1,0:T(8,128)S(1)}, f32[2,8,512]{2,1,0:T(8,128)}, u32[]{:S(2)}, u32[]{:S(2)}) %collective-permute-start.7) | collective-permute-done | bytes 32800 | tf_op jit(solution)/shard_map/cond/branch_1_fun/ppermute | solution.py:169
  52.1 1.8 %collective-permute-done.6 = f32[2,8,512]{2,1,0:T(8,128)} collective-permute-done((f32[2,8,512]{2,1,0:T(8,128)S(1)}, f32[2,8,512]{2,1,0:T(8,128)}, u32[]{:S(2)}, u32[]{:S(2)}) %collective-permute-start.6) | collective-permute-done | bytes 32800 | tf_op jit(solution)/shard_map/cond/branch_1_fun/ppermute | solution.py:167
  53.9 0.0 collective-permute-done.4.refs_2_
  53.9 2.4 %pack.3 = (bf16[8,96,512]{2,1,0:T(8,128)(2,1)}, bf16[8,96,512]{2,1,0:T(8,128)(2,1)S(1)}) custom-call(s32[2]{0:T(128)S(1)} %get-tuple-element.20.place, bf16[272,512]{1,0:T(8,128)(2,1)S(1)} %collective-permute-done.2.refs_0_, bf16[272,512]{1,0:T(8,128)(2,1)S(1)} %collective-permute-done.3.refs_1_, bf16[272,512]{1,0:T(8,128)(2,1)S(1)} %collective-permute-done.4.refs_2_), custom_call_target="tpu_custom_call" | custom-call | flops 1200000000 | bytes 1024 | tf_op jit(solution)/shard_map/cond/branch_1_fun/pack/pallas_call | solution.py:243
  56.3 0.0 collective-permute-start.9
  56.3 2.4 %collective-permute-done.9 = bf16[8,96,512]{2,1,0:T(8,128)(2,1)} collective-permute-done((bf16[8,96,512]{2,1,0:T(8,128)(2,1)S(1)}, bf16[8,96,512]{2,1,0:T(8,128)(2,1)}, u32[]{:S(2)}, u32[]{:S(2)}) %collective-permute-start.9) | collective-permute-done | bytes 786464 | tf_op jit(solution)/shard_map/cond/branch_1_fun/ppermute | solution.py:312
  58.7 0.0 all-to-all-done.refs_4_
  58.7 3.5 %partial.1 = s16[8,2,128,512]{3,2,1,0:T(8,128)(2,1)S(1)} custom-call(s32[2]{0:T(128)S(1)} %pad_add_fusion.place, bf16[8,160,512]{2,1,0:T(8,128)(2,1)S(1)} %get-tuple-element.58.refs_0_, bf16[8,96,512]{2,1,0:T(8,128)(2,1)} %get-tuple-element.59.refs_1_, bf16[8,160,512]{2,1,0:T(8,128)(2,1)} %get-tuple-element.60.refs_2_, ...), custom_call_target="tpu_custom_call" | custom-call | flops 1074000000 | bytes 8388608 | tf_op jit(solution)/shard_map/partial/pallas_call | solution.py:269
  62.3 0.0 slice-start.1
  62.3 33.7 %all_to_all.10 = s16[16,128,512]{2,1,0:T(8,128)(2,1)S(1)} all-to-all(s16[16,128,512]{2,1,0:T(8,128)(2,1)S(1)} %bitcast.27), channel_id=1, replica_groups=mesh['z'=8,'x'=4,'yh'=2,'c'=2,'yl'=2] {'x','yh','yl'}, dimensions={0} | all-to-all | bytes 4194304 | tf_op jit(solution)/shard_map/all_to_all | solution.py:359
  96.0 0.3 convert_reduce_fusion
  96.2 0.0 copy-start.2
  96.3 0.1 collective-permute-start.12
  96.4 2.1 %collective-permute-start.13 = (s16[32,1024]{1,0:T(8,128)(2,1)S(1)}, s16[32,1024]{1,0:T(8,128)(2,1)S(1)}, u32[]{:S(2)}, u32[]{:S(2)}) collective-permute-start(s16[32,1024]{1,0:T(8,128)(2,1)S(1)} %fusion.7), channel_id=1, source_target_pairs={{0,255},{1,0},{2,1},{3,2},{4,3},{5,4},{6,5},{7,6},{8,7},{9,8},{10,... | collective-permute-start | bytes 196616 | tf_op jit(solution)/shard_map/ppermute | solution.py:160
  98.5 0.3 sums.1.code
  98.8 2.1 %collective-permute-done.12.code_left = s16[32,1024]{1,0:T(8,128)(2,1)S(1)} collective-permute-done((s16[32,1024]{1,0:T(8,128)(2,1)S(1)}, s16[32,1024]{1,0:T(8,128)(2,1)S(1)}, u32[]{:S(2)}, u32[]{:S(2)}) %collective-permute-start.12) | collective-permute-done | bytes 65568 | tf_op jit(solution)/shard_map/ppermute | solution.py:160
  101.0 8.7 %march.1 = (f32[2,32,512]{2,1,0:T(8,128)S(1)}, bf16[2,32,512]{2,1,0:T(8,128)(2,1)S(1)}) custom-call(s32[1]{0:T(128)} %bitcast.6.side, s32[128,1024]{1,0:T(8,128)S(1)} %sums.1.code, s16[32,1024]{1,0:T(8,128)(2,1)S(1)} %collective-permute-done.12.code_left, s16[32,1024]{1,0:T(8,128)(2,1)S(1)} %collective-permute-done.13.code_right, ...), custom_call_target="tpu_custom_call" | custom-call | flops 3221225472 | bytes 10485760 | tf_op jit(solution)/shard_map/march/pallas_call | solution.py:116
  109.6 6.2 %collective-permute-start.14 = (bf16[2,32,512]{2,1,0:T(8,128)(2,1)S(1)}, bf16[2,32,512]{2,1,0:T(8,128)(2,1)S(1)}, u32[]{:S(2)}, u32[]{:S(2)}) collective-permute-start(bf16[2,32,512]{2,1,0:T(8,128)(2,1)S(1)} %get-tuple-element.67), channel_id=1, source_target_pairs={{0,1},{1,0},{2,3},{3,2},{4,5},{5,4},{6,7},{7,6},{8,9},{9,8},{10,11... | collective-permute-start | bytes 196616 | tf_op jit(solution)/shard_map/ppermute | solution.py:156
  115.8 2.2 %collective-permute-done.14.other = bf16[2,32,512]{2,1,0:T(8,128)(2,1)S(1)} collective-permute-done((bf16[2,32,512]{2,1,0:T(8,128)(2,1)S(1)}, bf16[2,32,512]{2,1,0:T(8,128)(2,1)S(1)}, u32[]{:S(2)}, u32[]{:S(2)}) %collective-permute-start.14) | collective-permute-done | bytes 65568 | tf_op jit(solution)/shard_map/ppermute | solution.py:156
  118.1 0.8 merge.1
  (27 shorter events, 0.1 us)
Async XLA Ops:
  2.7 10.0 %copy-start.3 = (bf16[272,512]{1,0:T(8,128)(2,1)}, bf16[272,512]{1,0:T(8,128)(2,1)S(1)}, u32[]{:S(2)}) copy-start(bf16[272,512]{1,0:T(8,128)(2,1)S(1)} %fusion.1) | copy-start | bytes 835588
  2.7 11.8 %collective-permute-start.11 = (bf16[272,512]{1,0:T(8,128)(2,1)S(1)}, bf16[272,512]{1,0:T(8,128)(2,1)S(1)}, u32[]{:S(2)}, u32[]{:S(2)}) collective-permute-start(bf16[272,512]{1,0:T(8,128)(2,1)S(1)} %fusion.1), channel_id=1, source_target_pairs={{0,224},{32,0},{64,32},{96,64},{128,96},{160,128},{192,160},{224,1... | collective-permute-start | bytes 835592 | tf_op jit(solution)/shard_map/ppermute | solution.py:308
  8.7 9.3 %collective-permute-start.10 = (bf16[272,512]{1,0:T(8,128)(2,1)S(1)}, bf16[272,512]{1,0:T(8,128)(2,1)S(1)}, u32[]{:S(2)}, u32[]{:S(2)}) collective-permute-start(bf16[272,512]{1,0:T(8,128)(2,1)S(1)} %fusion.1), channel_id=1, source_target_pairs={{0,32},{32,64},{64,96},{96,128},{128,160},{160,192},{192,224},{224... | collective-permute-start | bytes 835592 | tf_op jit(solution)/shard_map/ppermute | solution.py:308
  8.7 1.6 %copy-start = (bf16[64,4,4096]{2,1,0:T(4,128)(2,1)S(1)}, bf16[64,4,4096]{2,1,0:T(4,128)(2,1)}, u32[]{:S(2)}) copy-start(bf16[64,4,4096]{2,1,0:T(4,128)(2,1)} %weights.1) | copy-start | bytes 6291460
  12.8 12.0 %copy-start.5 = (s32[1,128]{1,0:T(1,128)S(1)}, s32[1,128]{1,0:T(1,128)}, u32[]{:S(2)}) copy-start(s32[1,128]{1,0:T(1,128)} %param.11) | copy-start | bytes 1540
  12.8 12.0 %copy-start.4 = (f32[64,2,512]{2,1,0:T(2,128)S(1)}, f32[64,2,512]{2,1,0:T(2,128)}, u32[]{:S(2)}) copy-start(f32[64,2,512]{2,1,0:T(2,128)} %param.8) | copy-start | bytes 786436
  14.6 3.4 %copy-start.6 = (bf16[272,512]{1,0:T(8,128)(2,1)}, bf16[272,512]{1,0:T(8,128)(2,1)S(1)}, u32[]{:S(2)}) copy-start(bf16[272,512]{1,0:T(8,128)(2,1)S(1)} %collective-permute-done.11) | copy-start | bytes 835588
  18.0 0.7 copy-start.7
  18.7 40.0 %all-to-all-start = ((bf16[8,256,512]{2,1,0:T(8,128)(2,1)}), bf16[8,256,512]{2,1,0:T(8,128)(2,1)S(1)}, u32[]{:S(2)}, u32[]{:S(2)}) async-start(bf16[8,256,512]{2,1,0:T(8,128)(2,1)} %sort.1), calls=%async_computation | async-start | bytes 4194304 | tf_op jit(solution)/shard_map/all_to_all | solution.py:352
  24.9 0.7 copy-start.1
  25.6 8.3 %collective-permute-start = (bf16[272,512]{1,0:T(8,128)(2,1)}, bf16[272,512]{1,0:T(8,128)(2,1)S(1)}, u32[]{:S(2)}, u32[]{:S(2)}) collective-permute-start(bf16[272,512]{1,0:T(8,128)(2,1)} %get-tuple-element.22.refs_1_), channel_id=1, source_target_pairs={{0,32},{32,64},{64,96},{96,128},{128,160},{160,192},{192,224},{224... | collective-permute-start | bytes 835592 | tf_op jit(solution)/shard_map/cond/branch_1_fun/ppermute | solution.py:308
  25.6 8.4 %collective-permute-start.1 = (bf16[272,512]{1,0:T(8,128)(2,1)}, bf16[272,512]{1,0:T(8,128)(2,1)S(1)}, u32[]{:S(2)}, u32[]{:S(2)}) collective-permute-start(bf16[272,512]{1,0:T(8,128)(2,1)} %get-tuple-element.23.refs_2_), channel_id=1, source_target_pairs={{0,224},{32,0},{64,32},{96,64},{128,96},{160,128},{192,160},{224,1... | collective-permute-start | bytes 835592 | tf_op jit(solution)/shard_map/cond/branch_1_fun/ppermute | solution.py:308
  33.9 7.8 %collective-permute-start.2 = (bf16[272,512]{1,0:T(8,128)(2,1)S(1)}, bf16[272,512]{1,0:T(8,128)(2,1)S(1)}, u32[]{:S(2)}, u32[]{:S(2)}) collective-permute-start(bf16[272,512]{1,0:T(8,128)(2,1)S(1)} %collective-permute-done.refs_3_), channel_id=1, source_target_pairs={{0,32},{32,64},{64,96},{96,128},{128,160},{160,192},{192,224},{224... | collective-permute-start | bytes 835592 | tf_op jit(solution)/shard_map/cond/branch_1_fun/ppermute | solution.py:308
  33.9 7.8 %collective-permute-start.3 = (bf16[272,512]{1,0:T(8,128)(2,1)S(1)}, bf16[272,512]{1,0:T(8,128)(2,1)S(1)}, u32[]{:S(2)}, u32[]{:S(2)}) collective-permute-start(bf16[272,512]{1,0:T(8,128)(2,1)S(1)} %collective-permute-done.1.refs_4_), channel_id=1, source_target_pairs={{0,224},{32,0},{64,32},{96,64},{128,96},{160,128},{192,160},{224,1... | collective-permute-start | bytes 835592 | tf_op jit(solution)/shard_map/cond/branch_1_fun/ppermute | solution.py:308
  41.7 12.3 %collective-permute-start.4 = (bf16[272,512]{1,0:T(8,128)(2,1)S(1)}, bf16[272,512]{1,0:T(8,128)(2,1)S(1)}, u32[]{:S(2)}, u32[]{:S(2)}) collective-permute-start(bf16[272,512]{1,0:T(8,128)(2,1)S(1)} %collective-permute-done.2.refs_0_), channel_id=1, source_target_pairs={{0,32},{32,64},{64,96},{96,128},{128,160},{160,192},{192,224},{224... | collective-permute-start | bytes 835592 | tf_op jit(solution)/shard_map/cond/branch_1_fun/ppermute | solution.py:308
  41.7 17.0 %collective-permute-start.8 = (bf16[8,160,512]{2,1,0:T(8,128)(2,1)S(1)}, bf16[8,160,512]{2,1,0:T(8,128)(2,1)}, u32[]{:S(2)}, u32[]{:S(2)}) collective-permute-start(bf16[8,160,512]{2,1,0:T(8,128)(2,1)S(1)} %get-tuple-element.33), channel_id=1, source_target_pairs={{0,2},{2,0},{1,3},{3,1},{4,6},{6,4},{5,7},{7,5},{8,10},{10,8},{9,1... | collective-permute-start | bytes 3932168 | tf_op jit(solution)/shard_map/cond/branch_1_fun/ppermute | solution.py:312
  41.7 12.2 %collective-permute-start.5 = (f32[2,40,512]{2,1,0:T(8,128)S(1)}, f32[2,40,512]{2,1,0:T(8,128)}, u32[]{:S(2)}, u32[]{:S(2)}) collective-permute-start(f32[2,40,512]{2,1,0:T(8,128)S(1)} %slice_select_fusion), channel_id=1, source_target_pairs={{0,1},{1,0},{2,3},{3,2},{4,5},{5,4},{6,7},{7,6},{8,9},{9,8},{10,11... | collective-permute-start | bytes 491528 | tf_op jit(solution)/shard_map/cond/branch_1_fun/ppermute | solution.py:156
  43.2 8.9 %collective-permute-start.7 = (f32[2,8,512]{2,1,0:T(8,128)S(1)}, f32[2,8,512]{2,1,0:T(8,128)}, u32[]{:S(2)}, u32[]{:S(2)}) collective-permute-start(f32[2,8,512]{2,1,0:T(8,128)S(1)} %get-tuple-element.70), channel_id=1, source_target_pairs={{0,2},{1,255},{2,4},{3,1},{4,6},{5,3},{6,8},{7,5},{8,10},{9,7},{10... | collective-permute-start | bytes 98312 | tf_op jit(solution)/shard_map/cond/branch_1_fun/ppermute | solution.py:169
  50.5 3.4 %collective-permute-start.6 = (f32[2,8,512]{2,1,0:T(8,128)S(1)}, f32[2,8,512]{2,1,0:T(8,128)}, u32[]{:S(2)}, u32[]{:S(2)}) collective-permute-start(f32[2,8,512]{2,1,0:T(8,128)S(1)} %get-tuple-element.71), channel_id=1, source_target_pairs={{0,255},{1,2},{2,1},{3,4},{4,3},{5,6},{6,5},{7,8},{8,7},{9,10},{10... | collective-permute-start | bytes 98312 | tf_op jit(solution)/shard_map/cond/branch_1_fun/ppermute | solution.py:167
  56.3 2.4 %collective-permute-start.9 = (bf16[8,96,512]{2,1,0:T(8,128)(2,1)S(1)}, bf16[8,96,512]{2,1,0:T(8,128)(2,1)}, u32[]{:S(2)}, u32[]{:S(2)}) collective-permute-start(bf16[8,96,512]{2,1,0:T(8,128)(2,1)S(1)} %get-tuple-element.34), channel_id=1, source_target_pairs={{0,2},{2,0},{1,3},{3,1},{4,6},{6,4},{5,7},{7,5},{8,10},{10,8},{9,1... | collective-permute-start | bytes 2359304 | tf_op jit(solution)/shard_map/cond/branch_1_fun/ppermute | solution.py:312
  58.7 42.2 %slice-start = ((s8[8388608]{0:T(1024)(128)(4,1)}), s8[4194304]{0:T(1024)(128)(4,1)S(1)}, s32[]{:S(2)}) async-start(s8[8388608]{0:T(1024)(128)(4,1)} %bitcast.28), calls=%async_computation.2 | async-start | bytes 8388608
  62.3 38.6 %slice-start.1 = ((s8[8388608]{0:T(1024)(128)(4,1)}), s8[4194304]{0:T(1024)(128)(4,1)S(1)}, s32[]{:S(2)}) async-start(s8[8388608]{0:T(1024)(128)(4,1)} %bitcast.28), calls=%async_computation.3 | async-start | bytes 8388608
  96.2 4.7 %copy-start.2 = (f32[64,2,512]{2,0,1:T(8,128)S(1)}, f32[64,2,512]{2,0,1:T(8,128)}, u32[]{:S(2)}) copy-start(f32[64,2,512]{2,0,1:T(8,128)} %copy-done.1) | copy-start | bytes 786436
  96.3 4.6 %collective-permute-start.12 = (s16[32,1024]{1,0:T(8,128)(2,1)S(1)}, s16[32,1024]{1,0:T(8,128)(2,1)S(1)}, u32[]{:S(2)}, u32[]{:S(2)}) collective-permute-start(s16[32,1024]{1,0:T(8,128)(2,1)S(1)} %fusion.4), channel_id=1, source_target_pairs={{0,1},{1,2},{2,3},{3,4},{4,5},{5,6},{6,7},{7,8},{8,9},{9,10},{10,1... | collective-permute-start | bytes 196616 | tf_op jit(solution)/shard_map/ppermute | solution.py:160
  96.4 4.5 %collective-permute-start.13 = (s16[32,1024]{1,0:T(8,128)(2,1)S(1)}, s16[32,1024]{1,0:T(8,128)(2,1)S(1)}, u32[]{:S(2)}, u32[]{:S(2)}) collective-permute-start(s16[32,1024]{1,0:T(8,128)(2,1)S(1)} %fusion.7), channel_id=1, source_target_pairs={{0,255},{1,0},{2,1},{3,2},{4,3},{5,4},{6,5},{7,6},{8,7},{9,8},{10,... | collective-permute-start | bytes 196616 | tf_op jit(solution)/shard_map/ppermute | solution.py:160
  109.6 8.4 %collective-permute-start.14 = (bf16[2,32,512]{2,1,0:T(8,128)(2,1)S(1)}, bf16[2,32,512]{2,1,0:T(8,128)(2,1)S(1)}, u32[]{:S(2)}, u32[]{:S(2)}) collective-permute-start(bf16[2,32,512]{2,1,0:T(8,128)(2,1)S(1)} %get-tuple-element.67), channel_id=1, source_target_pairs={{0,1},{1,0},{2,3},{3,2},{4,5},{5,4},{6,7},{7,6},{8,9},{9,8},{10,11... | collective-permute-start | bytes 196616 | tf_op jit(solution)/shard_map/ppermute | solution.py:156
